TPU v7x, 128 devices: a whole 4x4x4 slice. The times are simulated.
128 devices in a mesh: table: 16 (over y, z), expert: 8 (over x, core).
Axes of the slice: x: 4, y: 4, z: 4, core: 2. Of those that a mesh axis runs over, the one named last changes fastest.
Arguments:
- emb_rows: bfloat16 [8192, 128], P('table'), may hold values from -3 to 3
- row_ids: int32 [16384, 8, 4], P(('table', 'expert')), may hold values from 0 to 8191
- route_ids: int32 [16384, 2], P(('table', 'expert')), may hold values from 0 to 7, all different within a row; in each aligned block of 128 rows (0 to 127, 128 to 255, ...) at most 48 rows name the same one
- route_gates: float32 [16384, 2], P(('table', 'expert')), may hold values from 0.1 to 1
- w_in: bfloat16 [8, 1024, 4096], P('expert'), may hold values from -0.1875 to 0.1875
- w_out: bfloat16 [8, 4096, 512], P('expert'), may hold values from -0.09375 to 0.09375
- tower_in: bfloat16 [512, 2048], replicated, may hold values from -0.25 to 0.25
- tower_out: float32 [8, 256], replicated, may hold values from -0.375 to 0.375
- labels: float32 [16384, 8], P(('table', 'expert')), may hold values from 0 to 1
Outputs:
- grad_rows: float32 [8192, 128], P(('table', 'expert'))
- grad_tower_in: float32 [512, 2048], replicated
- grad_tower_out: float32 [8, 256], replicated
Inputs may be any that keep to these rules, and one draw needn't show every extreme that they name: `route_ids`: among the rows of one device, no expert is named by more than 48 rows, a bound that some block reaches; a row names two different experts.
All inputs are finite; a program needn't handle non-finite values.
Results may differ from a plain program's by a relative error of at most 0.015.
Values may be sent and summed in bfloat16 or wider, within the bound.
A program may use at most 128 MiB of HBM per device.

v0:
```python
import jax
import jax.numpy as jnp
from jax import lax
from jax.sharding import PartitionSpec as P


def silu_grad(pre):
    sig = jax.nn.sigmoid(pre)
    return sig * (1.0 + pre * (1.0 - sig))


def bag_counts(ids_one, offset, limit):
    local = ids_one - offset
    column = jnp.arange(limit, dtype=jnp.int32)
    hits = (local[:, :, None] == column[None, None, :]).astype(jnp.float32)
    return jnp.sum(hits, axis=1).astype(jnp.bfloat16)


def pool_owned(table_rows, ids, offset):
    limit = table_rows.shape[0]
    per_table = jnp.moveaxis(ids, 1, 0)

    def one_table(ids_one):
        counts = bag_counts(ids_one, offset, limit)
        return jnp.dot(counts, table_rows, preferred_element_type=jnp.float32)

    pooled = lax.map(one_table, per_table)
    return jnp.moveaxis(pooled, 0, 1)


def move_slots(boxes):
    return lax.all_to_all(boxes, "expert", split_axis=0, concat_axis=0, tiled=True)


def per_device(emb_rows, row_ids, route_ids, route_gates, w_in, w_out, tower_in, tower_out, labels):
    row_dev, dim = emb_rows.shape
    samples, tables, bag = row_ids.shape
    width = tables * dim
    groups = lax.axis_size("expert")
    capacity = 3 * samples // groups
    shard = lax.axis_index("table")
    tasks, tower_width = tower_out.shape
    eout = w_out.shape[2]
    all_ids = lax.all_gather(row_ids, "table", axis=0, tiled=True)
    pooled = lax.psum_scatter(
        pool_owned(emb_rows, all_ids, shard * row_dev), "table", scatter_dimension=0, tiled=True
    )
    tokens = pooled.reshape(samples, width).astype(jnp.bfloat16)
    flat = route_ids.reshape(-1)
    onehot = (flat[:, None] == jnp.arange(groups, dtype=jnp.int32)[None, :]).astype(jnp.int32)
    position = jnp.sum((jnp.cumsum(onehot, axis=0) - onehot) * onehot, axis=1)
    slot_index = flat * capacity + position
    slot_range = jnp.arange(groups * capacity, dtype=jnp.int32)
    placing = (slot_index[:, None] == slot_range[None, :]).astype(jnp.bfloat16)
    by_sample = jnp.sum(
        placing.reshape(samples, 2, groups * capacity).astype(jnp.float32), axis=1
    ).astype(jnp.bfloat16)
    outbox = jnp.einsum("bs,bf->sf", by_sample, tokens, preferred_element_type=jnp.float32).astype(
        jnp.bfloat16
    )
    inbox = move_slots(outbox.reshape(groups, capacity, width)).reshape(groups * capacity, width)
    pre = jnp.dot(inbox, w_in[0], preferred_element_type=jnp.float32)
    hidden = jax.nn.silu(pre).astype(jnp.bfloat16)
    produced = jnp.dot(hidden, w_out[0], preferred_element_type=jnp.float32).astype(jnp.bfloat16)
    returned = move_slots(produced.reshape(groups, capacity, eout)).reshape(groups * capacity, eout)
    expert_out = jnp.dot(placing, returned, preferred_element_type=jnp.float32).reshape(
        samples, 2, eout
    )
    combined = jnp.sum(route_gates[:, :, None] * expert_out, axis=1).astype(jnp.bfloat16)
    tower_pre = jnp.dot(combined, tower_in, preferred_element_type=jnp.float32)
    units = jax.nn.silu(tower_pre).reshape(samples, tasks, tower_width)
    logits = jnp.sum(units * tower_out[None, :, :], axis=2)
    dlogits = (jax.nn.sigmoid(logits) - labels) / tasks
    local_out = jnp.einsum("bk,bki->ki", dlogits, units)
    dunits = dlogits[:, :, None] * tower_out[None, :, :]
    dtower = (dunits.reshape(samples, tasks * tower_width) * silu_grad(tower_pre)).astype(
        jnp.bfloat16
    )
    local_in = jnp.einsum("bd,bh->dh", combined, dtower, preferred_element_type=jnp.float32)
    grad_tower_in, grad_tower_out = lax.psum((local_in, local_out), ("table", "expert"))
    dcombined = jnp.einsum("bh,dh->bd", dtower, tower_in, preferred_element_type=jnp.float32)
    dentries = (
        (route_gates[:, :, None] * dcombined[:, None, :])
        .astype(jnp.bfloat16)
        .reshape(samples * 2, eout)
    )
    doutbox = jnp.einsum("ns,ne->se", placing, dentries, preferred_element_type=jnp.float32).astype(
        jnp.bfloat16
    )
    dinbox = move_slots(doutbox.reshape(groups, capacity, eout)).reshape(groups * capacity, eout)
    dhidden = jnp.einsum("ce,he->ch", dinbox, w_out[0], preferred_element_type=jnp.float32)
    dpre = (dhidden * silu_grad(pre)).astype(jnp.bfloat16)
    drows = jnp.einsum("ch,fh->cf", dpre, w_in[0], preferred_element_type=jnp.float32).astype(
        jnp.bfloat16
    )
    dback = move_slots(drows.reshape(groups, capacity, width)).reshape(groups * capacity, width)
    dentry = jnp.dot(placing, dback, preferred_element_type=jnp.float32).reshape(samples, 2, width)
    dpooled = jnp.sum(dentry, axis=1).astype(jnp.bfloat16).reshape(samples, tables, dim)
    group_grads = lax.all_gather(dpooled, "table", axis=0, tiled=True)
    ids_by_table = jnp.moveaxis(all_ids, 1, 0)
    grads_by_table = jnp.moveaxis(group_grads, 1, 0)

    def add_table(total, inputs):
        ids_one, grads_one = inputs
        counts = bag_counts(ids_one, shard * row_dev, row_dev)
        term = jnp.einsum("nr,nd->rd", counts, grads_one, preferred_element_type=jnp.float32)
        return (total + term, None)

    sums, unused = lax.scan(
        add_table, jnp.zeros((row_dev, dim), jnp.float32), (ids_by_table, grads_by_table)
    )
    grad_rows = lax.psum_scatter(
        sums.astype(jnp.bfloat16), "expert", scatter_dimension=0, tiled=True
    ).astype(jnp.float32)
    return (grad_rows, grad_tower_in, grad_tower_out)


def solution(mesh):
    return jax.shard_map(
        per_device,
        mesh=mesh,
        in_specs=(
            P("table", None),
            P(("table", "expert"), None, None),
            P(("table", "expert"), None),
            P(("table", "expert"), None),
            P("expert", None, None),
            P("expert", None, None),
            P(),
            P(),
            P(("table", "expert"), None),
        ),
        out_specs=(P(("table", "expert"), None), P(), P()),
        check_vma=False,
    )
```

profile of v0, /device:TPU:0, one launch (start us, length us, event | category | flops | bytes accessed | tf_op | source)
XLA Modules:
  0.0 559.5 jit_solution(17748893278553555009)
XLA Ops:
  7.2 25.7 %all_gather.6 = s32[2048,8,4]{0,2,1:T(4,128)S(1)} all-gather(s32[128,8,4]{0,2,1:T(4,128)} %param.14), channel_id=1, replica_groups=mesh['table'=16,'expert'=8] {'table'}, dimensions={0}, use_global_device_ids=true | all-gather | bytes 278528 | tf_op jit(solution)/shard_map/all_gather | solution.py:44
  32.9 42.8 %while.23 = (s32[]{:T(128)}, f32[8,2048,128]{1,2,0:T(8,128)}, s32[8,2048,4]{1,2,0:T(4,128)S(1)}, s32[]{:T(128)}, bf16[512,128]{1,0:T(8,128)(2,1)}, /*index=5*/s32[]{:T(128)}) while((s32[]{:T(128)}, f32[8,2048,128]{1,2,0:T(8,128)}, s32[8,2048,4]{1,2,0:T(4,128)S(1)}, s32[]{:T(128)}, bf16[512,128]{1,0:T(8,128)(2,1)}, /*index=5*/s32[]{:T(128)}) %tuple.67), condition=%wide.region_6.7_spmd, body=%wide.region_4.6_spmd.sunk | while | flops 279977984 | bytes 5472845 | solution.py:27
  33.0 2.6 convert_reduce_fusion.4
  35.6 2.7 fusion.76
  38.3 2.6 convert_reduce_fusion.4
  40.9 2.8 fusion.76
  43.7 2.6 convert_reduce_fusion.4
  46.3 2.7 fusion.76
  49.0 2.6 convert_reduce_fusion.4
  51.6 2.7 fusion.76
  54.4 2.6 convert_reduce_fusion.4
  57.0 2.7 fusion.76
  59.7 2.6 convert_reduce_fusion.4
  62.3 2.8 fusion.76
  65.1 2.6 convert_reduce_fusion.4
  67.7 2.7 fusion.76
  70.4 2.6 convert_reduce_fusion.4
  73.0 2.7 fusion.76
  75.8 0.7 copy-done.3
  76.8 0.6 reduce-window.6
  78.1 82.2 %reduce-scatter.3.cloned.1.call-done = f32[128,8,128]{0,2,1:T(8,128)} async-done(((f32[2048,8,128]{0,2,1:T(8,128)}), f32[128,8,128]{0,2,1:T(8,128)}) %reduce-scatter.3.cloned.1.call-update) | async-done | bytes 524304 | tf_op jit(solution)/shard_map/reduce_scatter | solution.py:45
  160.4 1.1 convert_element_type.79
  161.9 17.3 %all_to_all.20 = bf16[8,48,1024]{2,1,0:T(8,128)(2,1)S(1)} all-to-all(bf16[8,48,1024]{2,1,0:T(8,128)(2,1)S(1)} %bitcast.110), channel_id=1, replica_groups=mesh['table'=16,'expert'=8] {'expert'}, dimensions={0} | all-to-all | bytes 1572864 | tf_op jit(solution)/shard_map/all_to_all | solution.py:32
  179.2 5.9 %fusion.12 = f32[384,4096]{1,0:T(8,128)S(1)} fusion(bf16[384,1024]{1,0:T(8,128)(2,1)S(1)} %bitcast.120, bf16[1,1024,4096]{2,1,0:T(8,128)(2,1)} %param.17), kind=kOutput, calls=%fused_computation.17 | convolution fusion | flops 3221225472 | bytes 15466496 | tf_op jit(solution)/shard_map/dot_general | solution.py:62
  185.2 2.8 fusion.24
  188.0 3.6 all-to-all-start.1
  191.9 8.5 %all-to-all-done.1 = bf16[8,48,512]{2,1,0:T(8,128)(2,1)S(1)} async-done(((bf16[8,48,512]{2,1,0:T(8,128)(2,1)}), bf16[8,48,512]{2,1,0:T(8,128)(2,1)S(1)}, u32[]{:S(2)}, u32[]{:S(2)}) %all-to-all-start.1) | async-done | bytes 393248 | tf_op jit(solution)/shard_map/all_to_all | solution.py:32
  200.8 1.4 fusion.31
  202.2 1.0 copy-done.1
  204.6 1.6 multiply_convert_fusion.5
  206.2 0.8 fusion.50
  207.0 1.0 mul.124
  208.0 1.4 mul.125
  209.4 0.4 convolution_convert_fusion.1
  209.8 11.3 %all_to_all.21 = bf16[8,48,512]{2,1,0:T(8,128)(2,1)S(1)} all-to-all(bf16[8,48,512]{2,1,0:T(8,128)(2,1)S(1)} %bitcast.114), channel_id=1, replica_groups=mesh['table'=16,'expert'=8] {'expert'}, dimensions={0} | all-to-all | bytes 786432 | tf_op jit(solution)/shard_map/all_to_all | solution.py:32
  221.1 12.9 %fusion.19 = bf16[384,1024]{1,0:T(8,128)(2,1)} fusion(bf16[1,1024,4096]{2,1,0:T(8,128)(2,1)} %param.17, f32[384,4096]{1,0:T(8,128)} %copy-done.7, bf16[384,512]{1,0:T(8,128)(2,1)S(1)} %bitcast.122, bf16[1,4096,512]{2,1,0:T(8,128)(2,1)} %param.18), kind=kOutput, calls=%fused_computation.25 | convolution fusion | flops 4846387200 | bytes 20054016 | tf_op jit(solution)/shard_map/ch,fh->cf/dot_general | solution.py:93
  234.1 16.7 %all_to_all.22 = bf16[8,48,1024]{2,1,0:T(8,128)(2,1)S(1)} all-to-all(bf16[8,48,1024]{2,1,0:T(8,128)(2,1)} %bitcast.118), channel_id=1, replica_groups=mesh['table'=16,'expert'=8] {'expert'}, dimensions={0} | all-to-all | bytes 1572864 | tf_op jit(solution)/shard_map/all_to_all | solution.py:32
  250.8 0.5 convolution_reduce_fusion
  251.3 0.8 copy.63
  252.2 55.2 %all-gather.2.cloned.1.call-done = bf16[2048,8,128]{0,2,1:T(8,128)(2,1)} async-done(((bf16[128,8,128]{0,2,1:T(8,128)(2,1)}), bf16[2048,8,128]{0,2,1:T(8,128)(2,1)}) %all-gather.2.cloned.1.call-update) | async-done | bytes 4194320 | tf_op jit(solution)/shard_map/all_gather | solution.py:99
  307.4 51.3 %while.24 = (s32[]{:T(128)}, f32[512,128]{1,0:T(8,128)S(1)}, s32[8,2048,4]{1,2,0:T(4,128)S(1)}, s32[]{:T(128)}, bf16[8,2048,128]{1,2,0:T(8,128)(2,1)}, /*index=5*/s32[]{:T(128)}, s32[]{:T(128)}) while((s32[]{:T(128)}, f32[512,128]{1,0:T(8,128)S(1)}, s32[8,2048,4]{1,2,0:T(4,128)S(1)}, s32[]{:T(128)}, ...), condition=%wide.region_13.14_spmd.clone, body=%wide.region_11.13_spmd.clone.sunk | while | flops 280109056 | bytes 5341791 | solution.py:109
  307.4 3.9 convert_reduce_fusion.5
  311.3 2.5 fusion.79
  313.8 3.9 convert_reduce_fusion.5
  317.7 2.5 fusion.79
  320.2 3.9 convert_reduce_fusion.5
  324.2 2.5 fusion.79
  326.6 3.9 convert_reduce_fusion.5
  330.6 2.5 fusion.79
  333.1 3.9 convert_reduce_fusion.5
  337.0 2.5 fusion.79
  339.5 3.9 convert_reduce_fusion.5
  343.4 2.5 fusion.79
  345.9 3.9 convert_reduce_fusion.5
  349.8 2.5 fusion.79
  352.3 3.9 convert_reduce_fusion.5
  356.2 2.5 fusion.79
  358.7 0.7 convert_element_type.92
  359.4 2.7 fusion.51
  362.2 1.4 fusion.28
  363.6 64.6 %psum.15 = f32[8,256]{1,0:T(8,128)} all-reduce(f32[8,256]{1,0:T(8,128)S(1)} %bitcast.126), channel_id=1, replica_groups=mesh['table'=16,'expert'=8] {'table','expert'}, use_global_device_ids=true, to_apply=%region_16.17 | all-reduce | flops 2048 | bytes 16384 | tf_op jit(solution)/shard_map/psum | solution.py:80
  428.2 1.3 convert_element_type.93
  429.6 118.7 %all-reduce.2.cloned.1.call-done = f32[512,2048]{1,0:T(8,128)} async-done(((f32[512,2048]{1,0:T(8,128)}), f32[512,2048]{1,0:T(8,128)}) %all-reduce.2.cloned.1.call-update) | async-done | bytes 4194320 | tf_op jit(solution)/shard_map/psum | solution.py:80
  548.3 4.7 copy.98
  (67 shorter events, 3.8 us)
Async XLA Ops:
  7.2 193.6 %copy-start = (bf16[512,2048]{1,0:T(8,128)(2,1)S(1)}, bf16[512,2048]{1,0:T(8,128)(2,1)}, u32[]{:S(2)}) copy-start(bf16[512,2048]{1,0:T(8,128)(2,1)} %param.19) | copy-start | bytes 6291460
  7.2 153.2 %reduce-scatter.3.cloned.1.call-start = ((), (), s32[]{:S(2)}) async-start(), calls=%async_computation.6 | async-start | bytes 8912896 | tf_op jit(solution)/shard_map/reduce_scatter | solution.py:45
  75.8 0.7 copy-start.3
  179.2 6.0 %copy-start.6 = (bf16[1,4096,512]{2,1,0:T(8,128)(2,1)S(1)}, bf16[1,4096,512]{2,1,0:T(8,128)(2,1)}, u32[]{:S(2)}) copy-start(bf16[1,4096,512]{2,1,0:T(8,128)(2,1)} %param.18) | copy-start | bytes 12582916
  185.2 2.8 copy-start.7
  185.2 6.5 %copy-start.2 = (f32[8,256]{1,0:T(8,128)S(1)}, f32[8,256]{1,0:T(8,128)}, u32[]{:S(2)}) copy-start(f32[8,256]{1,0:T(8,128)} %param.20) | copy-start | bytes 24580
  185.2 6.5 %copy-start.5 = (f32[128,2]{0,1:T(2,128)S(1)}, f32[128,2]{0,1:T(2,128)}, u32[]{:S(2)}) copy-start(f32[128,2]{0,1:T(2,128)} %param.16) | copy-start | bytes 3076
  188.0 15.9 %copy-start.4 = (f32[128,8]{0,1:T(8,128)S(1)}, f32[128,8]{0,1:T(8,128)}, u32[]{:S(2)}) copy-start(f32[128,8]{0,1:T(8,128)} %param.21) | copy-start | bytes 12292
  188.0 12.5 %all-to-all-start.1 = ((bf16[8,48,512]{2,1,0:T(8,128)(2,1)}), bf16[8,48,512]{2,1,0:T(8,128)(2,1)S(1)}, u32[]{:S(2)}, u32[]{:S(2)}) async-start(bf16[8,48,512]{2,1,0:T(8,128)(2,1)} %bitcast.12), calls=%async_computation.2 | async-start | bytes 786432 | tf_op jit(solution)/shard_map/all_to_all | solution.py:32
  191.6 115.8 %all-gather.2.cloned.1.call-start = ((), (), s32[]{:S(2)}) async-start(), calls=%async_computation.7 | async-start | bytes 4456448 | tf_op jit(solution)/shard_map/all_gather | solution.py:99
  202.2 1.0 copy-start.1
  252.1 176.1 %reduce-scatter.5.cloned.1.call-start = ((), (), s32[]{:S(2)}) async-start(), calls=%async_computation.8 | async-start | bytes 147456 | tf_op jit(solution)/shard_map/reduce_scatter | solution.py:112
  359.4 188.9 %all-reduce.2.cloned.1.call-start = ((), (), s32[]{:S(2)}) async-start(), calls=%async_computation.9 | async-start | bytes 8388608 | tf_op jit(solution)/shard_map/psum | solution.py:80
Sparse Core Ops, SparseCore 0:
  75.9 84.4 reduce-scatter.2
  252.2 55.1 all-gather.1
  359.5 29.5 reduce-scatter.4
  395.2 153.0 all-reduce.1
where the time goes:
time: 561 us; the launch traced here: 560 us
  waiting for transfers between devices  265 us (47%)
  blocking collectives  136 us (24%)
  matrix products  71.2 us (13%)
  other arithmetic  58.1 us (10%)
  between operations  14 us (2%)
  local copies, waits for them, and re-layouts  11.7 us (2%)
    psum x1, waiting for transfers between devices, per_device(): lax.psum((local_in, local_out), ('table', 'expert'))  119 us
    reduce_scatter x1, waiting for transfers between devices, per_device(): lax.psum_scatter(pool_owned(emb_rows, all_ids, shard * row_dev), 'table',...  82.2 us
    psum x1, blocking collectives, per_device(): lax.psum((local_in, local_out), ('table', 'expert'))  64.6 us
    all_gather x1, waiting for transfers between devices, per_device(): group_grads = lax.all_gather(dpooled, 'table', axis=0, tiled=True)  55.2 us
    reduce_sum x16, other arithmetic, bag_counts(): return jnp.sum(hits, axis=1).astype(jnp.bfloat16)  52.1 us
    all_to_all x3, blocking collectives, move_slots(): lax.all_to_all(boxes, 'expert', split_axis=0, concat_axis=0, tiled=True)  45.4 us
    all_gather x1, blocking collectives, per_device(): all_ids = lax.all_gather(row_ids, 'table', axis=0, tiled=True)  25.7 us
    dot_general x8, matrix products, one_table(): return jnp.dot(counts, table_rows, preferred_element_type=jnp.float32)  21.9 us
  transfers between devices with their start and end apart: 5, of which 4 were waited for; matrix products, arithmetic and copies ran while one was open for 1% of the time, Pallas kernels for 0%

commit v1 on v0

v1 whole, which is shorter than its diff:
```python
import functools

import jax
import jax.numpy as jnp
from jax import lax
from jax.experimental import pallas as pl
from jax.experimental.pallas import tpu as pltpu
from jax.sharding import PartitionSpec as P

MESH = pl.DeviceIdType.MESH
F32 = jnp.float32
BF16 = jnp.bfloat16
LANES = 128
HALVES = 2
CHUNK = 256
TILE = 512


def dot(a, b):
    return lax.dot_general(a, b, (((1,), (0,)), ((), ())), preferred_element_type=F32)


def dot_nt(a, b):
    return lax.dot_general(a, b, (((1,), (1,)), ((), ())), preferred_element_type=F32)


def silu_grad(pre, sig):
    return sig * (1.0 + pre * (1.0 - sig))


def kernel(
    n_table,
    n_expert,
    ids_ref,
    emb_ref,
    route_ref,
    gate_ref,
    labels_ref,
    tout_ref,
    w_in_hbm,
    w_out_hbm,
    tin_hbm,
    grows_ref,
    gin_hbm,
    gtout_ref,
    w_in,
    w_out,
    tin,
    ids,
    counts,
    rows,
    part_out,
    part_in,
    tokens,
    place,
    place_sum,
    place_t,
    place_both_t,
    outbox,
    inbox,
    acc,
    slope,
    made,
    returned,
    comb,
    dtow,
    dtow_own,
    comb_t,
    tower_out_box,
    tower_in_box,
    tower_x_out,
    tower_x_in,
    gin,
    gto_box,
    gto_mid,
    gto_last,
    dout,
    din,
    dpre,
    drows,
    dback,
    dpooled_t,
    gsend,
    grecv,
    gx_out,
    gx_in,
    wsem,
    loc_sem,
    sib_s,
    sib_r,
    emb_s,
    emb_r,
    box_s,
    box_r,
    back_s,
    back_r,
    dbox_s,
    dbox_r,
    dback_s,
    dback_r,
    tw_s,
    tw_r,
    twx_s,
    twx_r,
    twg_s,
    twg_r,
    twa_s,
    twa_r,
    gto_s,
    gto_r,
    gto2_s,
    gto2_r,
    g_s,
    g_r,
    gx_s,
    gx_r,
):
    t = lax.axis_index("table")
    e = lax.axis_index("expert")
    n_x = n_expert // 2
    x = e // 2
    core = e % 2
    sib = 1 - core
    batch = ids_ref.shape[0]
    lookups = ids_ref.shape[1]
    n_feat = tokens.shape[1] // LANES
    bag = lookups // n_feat
    cap = inbox.shape[1]
    slots = n_expert * cap
    width = tokens.shape[1]
    hid = w_in.shape[1]
    eout = w_out.shape[1]
    tasks, tw = tout_ref.shape
    per = emb_ref.shape[2]
    span = n_x * per
    cols = n_table * span
    n_chunks = width // CHUNK
    rel_per = n_expert // HALVES

    def rel_expert(i):
        return lax.rem(x + i // 2, n_x) * 2 + lax.rem(core + lax.rem(i, 2), 2)

    def rel_back(i):
        return lax.rem(n_x - i // 2, n_x) * 2 + lax.rem(i, 2)

    def remote(src, dst, ssem, rsem, to_t, to_e):
        return pltpu.make_async_remote_copy(
            src_ref=src, dst_ref=dst, send_sem=ssem, recv_sem=rsem,
            device_id=(to_t, to_e), device_id_type=MESH,
        )

    def to_sibling(src, dst, k):
        return remote(src, dst, sib_s.at[k], sib_r.at[k], t, x * 2 + sib)

    def fan_table(src, dst, ssem, rsem):
        def copy(i, at):
            peer = lax.rem(t + i, n_table)
            return remote(src(peer), dst(at(peer)), ssem.at[i], rsem.at[at(peer)], peer, e)

        def start():
            @pl.loop(1, n_table)
            def _(i):
                copy(i, lambda peer: t).start()

        def wait_recv():
            @pl.loop(1, n_table)
            def _(i):
                copy(i, lambda peer: peer).wait_recv()

        def wait_send():
            @pl.loop(1, n_table)
            def _(i):
                copy(i, lambda peer: t).wait_send()

        return start, wait_recv, wait_send

    def fan_x(src, dst, ssem, rsem):
        def copy(i, at):
            peer = lax.rem(x + i, n_x)
            return remote(src(peer), dst(at(peer)), ssem.at[i], rsem.at[at(peer)], t, peer * 2 + core)

        def start():
            @pl.loop(1, n_x)
            def _(i):
                copy(i, lambda peer: x).start()

        def wait_recv():
            @pl.loop(1, n_x)
            def _(i):
                copy(i, lambda peer: peer).wait_recv()

        def wait_send():
            @pl.loop(1, n_x)
            def _(i):
                copy(i, lambda peer: x).wait_send()

        return start, wait_recv, wait_send

    w_in_copy = pltpu.make_async_copy(w_in_hbm, w_in, wsem.at[0])
    w_out_copy = pltpu.make_async_copy(w_out_hbm, w_out, wsem.at[1])
    tin_copy = pltpu.make_async_copy(tin_hbm, tin, wsem.at[2])
    w_in_copy.start()
    w_out_copy.start()
    tin_copy.start()

    barrier = pltpu.get_barrier_semaphore()

    @pl.loop(1, n_table)
    def _(i):
        pl.semaphore_signal(barrier, inc=1, device_id=(lax.rem(t + i, n_table), e), device_id_type=MESH)

    @pl.loop(1, n_expert)
    def _(i):
        pl.semaphore_signal(barrier, inc=1, device_id=(t, lax.rem(e + i, n_expert)), device_id_type=MESH)

    ids[0] = jnp.zeros((batch, LANES), jnp.int32)
    ids[0, :, 0:lookups] = ids_ref[...]
    rows[t] = emb_ref[:, core].reshape(span, LANES)
    pl.semaphore_wait(barrier, n_table + n_expert - 2)

    ids_copy = to_sibling(ids.at[0], ids.at[1], 0)
    ids_copy.start()
    emb_start, emb_recv, emb_send = fan_table(lambda p: rows.at[t], lambda s: rows.at[s], emb_s, emb_r)
    emb_start()

    lane = lax.broadcasted_iota(jnp.int32, (batch, LANES), 1)
    slot_lane = lax.broadcasted_iota(jnp.int32, (batch, slots), 1)
    r0, r1 = route_ref[:, 0:1], route_ref[:, 1:2]
    named0, named1 = lane == r0, lane == r1
    named = jnp.where(named0 | named1, 1.0, 0.0).astype(BF16)
    earlier = jnp.where(
        lax.broadcasted_iota(jnp.int32, (batch, batch), 1) < lax.broadcasted_iota(jnp.int32, (batch, batch), 0),
        1.0, 0.0,
    ).astype(BF16)
    before = dot(earlier, named)
    placed = []
    for j, (r, hit) in enumerate(((r0, named0), (r1, named1))):
        pos = jnp.sum(jnp.where(hit, before, 0.0), axis=1, keepdims=True).astype(jnp.int32)
        placed.append(jnp.where(slot_lane == r * cap + pos, 1.0, 0.0))
        place[j] = placed[j].astype(BF16)
        place_both_t[:, j * batch : (j + 1) * batch] = placed[j].T.astype(BF16)
    both = placed[0] + placed[1]
    place_sum[...] = both.astype(BF16)
    place_t[...] = both.T.astype(BF16)

    @pl.loop(0, 2)
    def _(s):
        @pl.when(s == 1)
        def _():
            ids_copy.wait_recv()

        own = ids[s]
        near = (own // (2 * per)) * per + lax.rem(own, per)
        code = jnp.where(lax.rem(own // per, 2) == core, near, -1)
        for f in range(n_feat):
            high = []
            for k in range(bag):
                c = f * bag + k
                gap = code[:, c : c + 1] - lane
                high.append(jnp.where(jnp.bitwise_and(gap, LANES - 1) == 0, gap >> 7, -1).astype(BF16))

            @pl.loop(0, cols // LANES, unroll=4)
            def _(h):
                mark = h.astype(F32).astype(BF16)
                total = jnp.where(high[0] == mark, 1.0, 0.0).astype(BF16)
                for k in range(1, bag):
                    total += jnp.where(high[k] == mark, 1.0, 0.0).astype(BF16)
                counts[s, f * batch : (f + 1) * batch, pl.ds(pl.multiple_of(h * LANES, LANES), LANES)] = total

    emb_recv()

    def partial(s, c):
        block = counts[s, pl.ds(pl.multiple_of(c * CHUNK, CHUNK), CHUNK), :]
        return dot(block, rows[...].reshape(cols, LANES))

    def part_copy(c):
        return to_sibling(part_out.at[c], part_in.at[c], 1 + c)

    @pl.loop(0, n_chunks)
    def _(c):
        part_out[c] = partial(1, c)
        part_copy(c).start()

    per_chunk = CHUNK // LANES

    @pl.loop(0, n_chunks)
    def _(c):
        mine = partial(0, c)
        part_copy(c).wait_recv()
        pooled = (mine + part_in[c]).astype(BF16)
        for f in range(per_chunk):
            tokens[:, pl.ds(pl.multiple_of(c * CHUNK + f * LANES, LANES), LANES)] = pooled[f * batch : (f + 1) * batch]

    outbox[...] = dot(place_t[...], tokens[...]).astype(BF16).reshape(n_expert, cap, width)

    def box_copy(i, sending):
        peer = rel_expert(i)
        at = rel_back(i) if sending else i
        return remote(outbox.at[peer], inbox.at[at], box_s.at[i], box_r.at[at], t, peer)

    @pl.loop(1, n_expert)
    def _(i):
        box_copy(i, True).start()

    inbox[0] = outbox[e]

    w_in_copy.wait()
    w_out_copy.wait()

    def back_copy(i, sending):
        peer = rel_expert(i)
        at = e if sending else peer
        return remote(made.at[i], returned.at[at], back_s.at[i], back_r.at[at], t, peer)

    m_rows = rel_per * cap

    @pl.loop(0, HALVES)
    def _(half):
        @pl.loop(0, rel_per)
        def _(k):
            i = half * rel_per + k

            @pl.when(i > 0)
            def _():
                box_copy(i, False).wait_recv()

        acc[...] = jnp.zeros_like(acc)

        @pl.loop(0, hid // TILE)
        def _(n):
            at = pl.ds(pl.multiple_of(n * TILE, TILE), TILE)
            block = inbox[pl.ds(half * rel_per, rel_per)].reshape(m_rows, width)
            pre = dot(block, w_in[:, at])
            sig = jax.nn.sigmoid(pre)
            slope[half, :, at] = silu_grad(pre, sig).astype(BF16)
            acc[...] += dot((pre * sig).astype(BF16), w_out[at, :])

        made[pl.ds(half * rel_per, rel_per)] = acc[...].astype(BF16).reshape(rel_per, cap, eout)

        @pl.loop(0, rel_per)
        def _(k):
            i = half * rel_per + k

            @pl.when(i > 0)
            def _():
                back_copy(i, True).start()

    returned[e] = made[0]
    tin_copy.wait()

    @pl.loop(1, n_expert)
    def _(i):
        back_copy(i, False).wait_recv()

    gate0, gate1 = gate_ref[:, 0:1], gate_ref[:, 1:2]
    answers = returned[...].reshape(slots, eout)
    combined = (gate0 * dot(place[0], answers) + gate1 * dot(place[1], answers)).astype(BF16)
    comb[0] = combined
    dcomb = jnp.zeros((batch, eout), F32)
    per_half = tasks // 2
    for k in range(tasks):
        pre = dot(combined, tin[:, k * tw : (k + 1) * tw])
        sig = jax.nn.sigmoid(pre)
        units = pre * sig
        out_row = tout_ref[k : k + 1, :]
        logit = jnp.sum(units * out_row, axis=1, keepdims=True)
        dlogit = (jax.nn.sigmoid(logit) - labels_ref[:, k : k + 1]) / tasks
        gto_box[t, k : k + 1, :] = jnp.sum(dlogit * units, axis=0, keepdims=True)
        grad = (dlogit * out_row * silu_grad(pre, sig)).astype(BF16)
        dtow[k // per_half, :, (k % per_half) * tw : (k % per_half + 1) * tw] = grad
        dcomb += dot_nt(grad, tin[:, k * tw : (k + 1) * tw])
    dent = jnp.concatenate([(gate0 * dcomb).astype(BF16), (gate1 * dcomb).astype(BF16)], axis=0)
    dout[...] = dot(place_both_t[...], dent).astype(BF16).reshape(n_expert, cap, eout)

    def dbox_copy(i, sending):
        peer = rel_expert(i)
        at = rel_back(i) if sending else i
        return remote(dout.at[peer], din.at[at], dbox_s.at[i], dbox_r.at[at], t, peer)

    @pl.loop(1, n_expert)
    def _(i):
        dbox_copy(i, True).start()

    din[0] = dout[e]

    k_comb = 1 + n_chunks
    comb_copy = to_sibling(comb.at[0], comb.at[1], k_comb)
    dtow_copy = to_sibling(dtow.at[sib], dtow_own.at[1], k_comb + 1)
    comb_copy.start()
    dtow_copy.start()
    gto_start, gto_recv, gto_send = fan_table(lambda p: gto_box.at[t], lambda s: gto_box.at[s], gto_s, gto_r)
    gto_start()
    dtow_own[0] = dtow[core]
    comb_copy.wait_recv()
    dtow_copy.wait_recv()
    comb_t[:, 0:batch] = comb[0].astype(F32).T.astype(BF16)
    comb_t[:, batch : 2 * batch] = comb[1].astype(F32).T.astype(BF16)
    t_rows = eout // n_table
    t_cols = tasks * tw // 2
    x_cols = t_cols // n_x
    group = LANES // t_rows
    sides = dtow_own[...].reshape(2 * batch, t_cols)

    @pl.loop(0, eout // LANES)
    def _(i):
        block = dot(comb_t[pl.ds(pl.multiple_of(i * LANES, LANES), LANES), :], dtow_own[...].reshape(2 * batch, t_cols))
        tower_out_box[pl.ds(i * group, group)] = block.astype(BF16).reshape(group, t_rows, t_cols)

    tw_start, tw_recv, tw_send = fan_table(
        lambda p: tower_out_box.at[p], lambda s: tower_in_box.at[s], tw_s, tw_r
    )
    tw_start()
    tower_in_box[t] = tower_out_box[t]

    @pl.loop(0, HALVES)
    def _(half):
        @pl.loop(0, rel_per)
        def _(k):
            i = half * rel_per + k

            @pl.when(i > 0)
            def _():
                dbox_copy(i, False).wait_recv()

        @pl.loop(0, hid // TILE)
        def _(n):
            at = pl.ds(pl.multiple_of(n * TILE, TILE), TILE)
            block = din[pl.ds(half * rel_per, rel_per)].reshape(m_rows, eout)
            dhid = dot_nt(block, w_out[at, :])
            dpre[half, :, at] = (dhid * slope[half, :, at].astype(F32)).astype(BF16)

    def dback_copy(c, i, sending):
        peer = rel_expert(i)
        at = e if sending else peer
        return remote(drows.at[c, i], dback.at[c, at], dback_s.at[c, i], dback_r.at[c, at], t, peer)

    @pl.loop(0, n_chunks)
    def _(c):
        at = pl.ds(pl.multiple_of(c * CHUNK, CHUNK), CHUNK)

        @pl.loop(0, HALVES)
        def _(half):
            block = dot_nt(dpre[half], w_in[at, :])
            drows[c, pl.ds(half * rel_per, rel_per)] = block.astype(BF16).reshape(rel_per, cap, CHUNK)

            @pl.loop(0, rel_per)
            def _(k):
                i = half * rel_per + k

                @pl.when(i > 0)
                def _():
                    dback_copy(c, i, True).start()

        dback[c, e] = drows[c, 0]

    tw_recv()
    total = tower_in_box[0].astype(F32)
    for s in range(1, n_table):
        total += tower_in_box[s].astype(F32)
    for k in range(n_x):
        tower_x_out[k] = total[:, k * x_cols : (k + 1) * x_cols].astype(BF16)
    twx_start, twx_recv, twx_send = fan_x(lambda p: tower_x_out.at[p], lambda s: tower_x_in.at[s], twx_s, twx_r)
    twx_start()
    tower_x_in[x] = tower_x_out[x]
    gto_recv()
    gsum = gto_box[0]
    for s in range(1, n_table):
        gsum += gto_box[s]
    gto_last[e] = gsum
    gto_mid[...] = gsum

    def gto2_copy(i, sending):
        peer = lax.rem(e + i, n_expert)
        at = e if sending else peer
        return remote(gto_mid, gto_last.at[at], gto2_s.at[i], gto2_r.at[at], t, peer)

    @pl.loop(1, n_expert)
    def _(i):
        gto2_copy(i, True).start()

    twx_recv()
    total = tower_x_in[0].astype(F32)
    for s in range(1, n_x):
        total += tower_x_in[s].astype(F32)

    def gin_rows(s):
        return pl.ds(pl.multiple_of(s * t_rows, t_rows), t_rows)

    def gin_block(s):
        return gin.at[core, gin_rows(t), pl.ds(pl.multiple_of(s * x_cols, x_cols), x_cols)]

    gin[core, gin_rows(t), pl.ds(pl.multiple_of(x * x_cols, x_cols), x_cols)] = total.astype(BF16)
    twg_start, twg_recv, twg_send = fan_x(lambda p: gin_block(x), gin_block, twg_s, twg_r)
    twg_start()
    twg_recv()
    twa_start, twa_recv, twa_send = fan_table(
        lambda p: gin.at[core, gin_rows(t)], lambda s: gin.at[core, gin_rows(s)], twa_s, twa_r
    )
    twa_start()

    def dpool_copy(c):
        k = k_comb + 2 + c
        at = pl.multiple_of(c * CHUNK, CHUNK)
        return to_sibling(
            dpooled_t.at[:, pl.ds(at, CHUNK)], dpooled_t.at[:, pl.ds(width + at, CHUNK)], k
        )

    @pl.loop(0, n_chunks)
    def _(c):
        @pl.loop(1, n_expert)
        def _(i):
            dback_copy(c, i, False).wait_recv()

        got = dot(place_sum[...], dback[c].reshape(slots, CHUNK)).astype(BF16).astype(F32)
        for f in range(per_chunk):
            at = pl.multiple_of(c * CHUNK + f * LANES, LANES)
            dpooled_t[:, pl.ds(at, LANES)] = got[:, f * LANES : (f + 1) * LANES].T.astype(BF16)
        dpool_copy(c).start()

    @pl.loop(0, n_chunks)
    def _(c):
        dpool_copy(c).wait_recv()

    def shard_grads(p):
        block = counts[:, :, pl.ds(pl.multiple_of(p * span, span), span)].reshape(2 * width, span)
        return dot(dpooled_t[...], block).astype(BF16)

    def g_copy(i, sending):
        peer = lax.rem(t + i, n_table)
        at = t if sending else peer
        return remote(gsend.at[peer], grecv.at[at], g_s.at[i], g_r.at[at], peer, e)

    @pl.loop(1, n_table)
    def _(i):
        peer = lax.rem(t + i, n_table)
        gsend[peer] = shard_grads(peer)
        g_copy(i, True).start()

    grecv[t] = shard_grads(t)

    twa_recv()
    gin_copy = to_sibling(gin.at[core], gin.at[core], k_comb + 2 + n_chunks)
    gin_copy.start()

    @pl.loop(1, n_expert)
    def _(i):
        gto2_copy(i, False).wait_recv()

    gsum = gto_last[0]
    for s in range(1, n_expert):
        gsum += gto_last[s]
    gtout_ref[...] = gsum

    to_sibling(gin.at[sib], gin.at[sib], k_comb + 2 + n_chunks).wait_recv()
    gin_outs = [
        pltpu.make_async_copy(gin.at[h], gin_hbm.at[:, pl.ds(h * t_cols, t_cols)], loc_sem.at[h]) for h in range(2)
    ]
    for copy in gin_outs:
        copy.start()

    @pl.loop(1, n_table)
    def _(i):
        g_copy(i, False).wait_recv()

    total = grecv[0].astype(F32)
    for s in range(1, n_table):
        total += grecv[s].astype(F32)
    gx_out[...] = total.T.astype(BF16).reshape(n_x, per, LANES)
    gx_start, gx_recv, gx_send = fan_x(lambda p: gx_out.at[p], lambda s: gx_in.at[s], gx_s, gx_r)
    gx_start()
    gx_in[x] = gx_out[x]
    gx_recv()
    total = gx_in[0].astype(F32)
    for s in range(1, n_x):
        total += gx_in[s].astype(F32)
    grows_ref[...] = total

    ids_copy.wait_send()
    emb_send()
    comb_copy.wait_send()
    dtow_copy.wait_send()
    gto_send()
    tw_send()
    twx_send()
    twg_send()
    twa_send()
    gin_copy.wait_send()
    gx_send()

    @pl.loop(0, n_chunks)
    def _(c):
        part_copy(c).wait_send()
        dpool_copy(c).wait_send()

        @pl.loop(1, n_expert)
        def _(i):
            dback_copy(c, i, True).wait_send()

    @pl.loop(1, n_expert)
    def _(i):
        box_copy(i, True).wait_send()
        back_copy(i, True).wait_send()
        dbox_copy(i, True).wait_send()
        gto2_copy(i, True).wait_send()

    @pl.loop(1, n_table)
    def _(i):
        g_copy(i, True).wait_send()

    for copy in gin_outs:
        copy.wait()


def per_device(emb_rows, row_ids, route_ids, route_gates, w_in, w_out, tower_in, tower_out, labels):
    n_table = lax.axis_size("table")
    n_expert = lax.axis_size("expert")
    n_x = n_expert // 2
    samples, tables, bag = row_ids.shape
    cap = 3 * samples // n_expert
    row_dev, dim = emb_rows.shape
    width = tables * dim
    hid, eout = w_out.shape[1:]
    tasks, tw = tower_out.shape
    per = row_dev // n_expert
    span = n_x * per
    cols = n_table * span
    slots = n_expert * cap
    n_chunks = width // CHUNK
    m_rows = slots // HALVES
    t_rows = eout // n_table
    t_cols = tasks * tw // 2
    x_cols = t_cols // n_x
    n_sib = 1 + n_chunks + 2 + n_chunks + 1
    vmem = pl.BlockSpec(memory_space=pltpu.VMEM)
    hbm = pl.BlockSpec(memory_space=pl.ANY)
    dma = pltpu.SemaphoreType.DMA
    scratch = [
        pltpu.VMEM((width, hid), BF16),
        pltpu.VMEM((hid, eout), BF16),
        pltpu.VMEM((eout, tasks * tw), BF16),
        pltpu.VMEM((2, samples, LANES), jnp.int32),
        pltpu.VMEM((2, width, cols), BF16),
        pltpu.VMEM((n_table, span, LANES), BF16),
        pltpu.VMEM((n_chunks, CHUNK, LANES), F32),
        pltpu.VMEM((n_chunks, CHUNK, LANES), F32),
        pltpu.VMEM((samples, width), BF16),
        pltpu.VMEM((2, samples, slots), BF16),
        pltpu.VMEM((samples, slots), BF16),
        pltpu.VMEM((slots, samples), BF16),
        pltpu.VMEM((slots, 2 * samples), BF16),
        pltpu.VMEM((n_expert, cap, width), BF16),
        pltpu.VMEM((n_expert, cap, width), BF16),
        pltpu.VMEM((m_rows, eout), F32),
        pltpu.VMEM((HALVES, m_rows, hid), BF16),
        pltpu.VMEM((n_expert, cap, eout), BF16),
        pltpu.VMEM((n_expert, cap, eout), BF16),
        pltpu.VMEM((2, samples, eout), BF16),
        pltpu.VMEM((2, samples, t_cols), BF16),
        pltpu.VMEM((2, samples, t_cols), BF16),
        pltpu.VMEM((eout, 2 * samples), BF16),
        pltpu.VMEM((n_table, t_rows, t_cols), BF16),
        pltpu.VMEM((n_table, t_rows, t_cols), BF16),
        pltpu.VMEM((n_x, t_rows, x_cols), BF16),
        pltpu.VMEM((n_x, t_rows, x_cols), BF16),
        pltpu.VMEM((2, eout, t_cols), BF16),
        pltpu.VMEM((n_table, tasks, tw), F32),
        pltpu.VMEM((tasks, tw), F32),
        pltpu.VMEM((n_expert, tasks, tw), F32),
        pltpu.VMEM((n_expert, cap, eout), BF16),
        pltpu.VMEM((n_expert, cap, eout), BF16),
        pltpu.VMEM((HALVES, m_rows, hid), BF16),
        pltpu.VMEM((n_chunks, n_expert, cap, CHUNK), BF16),
        pltpu.VMEM((n_chunks, n_expert, cap, CHUNK), BF16),
        pltpu.VMEM((LANES, 2 * width), BF16),
        pltpu.VMEM((n_table, LANES, span), BF16),
        pltpu.VMEM((n_table, LANES, span), BF16),
        pltpu.VMEM((n_x, per, LANES), BF16),
        pltpu.VMEM((n_x, per, LANES), BF16),
        dma((3,)),
        dma((2,)),
        dma((n_sib,)),
        dma((n_sib,)),
        dma((n_table,)),
        dma((n_table,)),
        dma((n_expert,)),
        dma((n_expert,)),
        dma((n_expert,)),
        dma((n_expert,)),
        dma((n_expert,)),
        dma((n_expert,)),
        dma((n_chunks, n_expert)),
        dma((n_chunks, n_expert)),
        dma((n_table,)),
        dma((n_table,)),
        dma((n_x,)),
        dma((n_x,)),
        dma((n_x,)),
        dma((n_x,)),
        dma((n_table,)),
        dma((n_table,)),
        dma((n_table,)),
        dma((n_table,)),
        dma((n_expert,)),
        dma((n_expert,)),
        dma((n_table,)),
        dma((n_table,)),
        dma((n_x,)),
        dma((n_x,)),
    ]
    grows, gin, gtout = pl.pallas_call(
        functools.partial(kernel, n_table, n_expert),
        out_shape=(
            jax.ShapeDtypeStruct((per, dim), F32),
            jax.ShapeDtypeStruct((eout, tasks * tw), BF16),
            jax.ShapeDtypeStruct((tasks, tw), F32),
        ),
        in_specs=[vmem] * 6 + [hbm] * 3,
        out_specs=(vmem, hbm, vmem),
        scratch_shapes=scratch,
        compiler_params=pltpu.CompilerParams(
            collective_id=0, has_side_effects=True, vmem_limit_bytes=VMEM_LIMIT
        ),
    )(
        row_ids.reshape(samples, tables * bag),
        emb_rows.reshape(n_x, 2, per, dim),
        route_ids,
        route_gates,
        labels,
        tower_out,
        w_in[0],
        w_out[0],
        tower_in,
    )
    return grows, gin.astype(F32), gtout


VMEM_LIMIT = 62 * 1024 * 1024


def solution(mesh):
    return jax.shard_map(
        per_device,
        mesh=mesh,
        in_specs=(
            P("table", None),
            P(("table", "expert"), None, None),
            P(("table", "expert"), None),
            P(("table", "expert"), None),
            P("expert", None, None),
            P("expert", None, None),
            P(),
            P(),
            P(("table", "expert"), None),
        ),
        out_specs=(P(("table", "expert"), None), P(), P()),
        check_vma=False,
    )
```

time: 561 us -> 160 us (0.29)
  waiting for transfers between devices: 265 us -> 0 us
  Pallas kernels: 0 us -> 148 us
  blocking collectives: 136 us -> 0 us
  matrix products: 71.2 us -> 0 us
  other arithmetic: 58.1 us -> 4.14 us
  between operations: 14 us -> 0.66 us
    pallas_call x0 -> x1, Pallas kernels: none -> 148 us  [per_device(): pl.pallas_call(functools.partial(kernel, n_table, n_expert), out_shape=(j...]
    psum x1 -> x0, waiting for transfers between devices: 119 us -> none  [per_device(): lax.psum((local_in, local_out), ('table', 'expert'))]
    reduce_scatter x2 -> x0, waiting for transfers between devices: 82.3 us -> none  [the longest x1 82.2 us: per_device(): lax.psum_scatter(pool_owned(emb_rows, all_ids, shard * row_dev), 'table',...]
    dot_general x27 -> x0, matrix products: 71.2 us -> none  [the longest x8 21.9 us: one_table(): return jnp.dot(counts, table_rows, preferred_element_type=jnp.float32)]
    psum x1 -> x0, blocking collectives: 64.6 us -> none  [per_device(): lax.psum((local_in, local_out), ('table', 'expert'))]
    all_gather x1 -> x0, waiting for transfers between devices: 55.2 us -> none  [per_device(): group_grads = lax.all_gather(dpooled, 'table', axis=0, tiled=True)]
    reduce_sum x19 -> x0, other arithmetic: 52.5 us -> none  [the longest x16 52.1 us: bag_counts(): return jnp.sum(hits, axis=1).astype(jnp.bfloat16)]
    all_to_all x3 -> x0, blocking collectives: 45.4 us -> none  [move_slots(): lax.all_to_all(boxes, 'expert', split_axis=0, concat_axis=0, tiled=True)]
  transfers between devices with their start and end apart: 5 -> 0, of which waited for: 4 -> 0; matrix products, arithmetic and copies ran while one was open for 1% -> 0% of each run, Pallas kernels for 0% -> 0%
where the time goes in v1:
time: 160 us; the launch traced here: 159 us
  Pallas kernels  148 us (92%)
  local copies, waits for them, and re-layouts  6.91 us (4%)
  other arithmetic  4.14 us (3%)
    pallas_call x1, Pallas kernels, per_device(): pl.pallas_call(functools.partial(kernel, n_table, n_expert), out_shape=(j...  148 us
    unnamed x9, local copies, waits for them, and re-layouts  5.46 us
    convert_element_type x1, other arithmetic, per_device(): return (grows, gin.astype(F32), gtout)  4.14 us

profile of v1, /device:TPU:0, one launch (start us, length us, event | category | flops | bytes accessed | tf_op | source)
XLA Modules:
  0.0 159.5 jit_solution(989227491597373565)
XLA Ops:
  0.6 1.4 copy.16.ids_ref
  2.1 1.4 copy.17.route_ref
  3.5 1.4 copy.18.gate_ref
  4.9 1.4 copy.19.labels_ref
  6.3 147.8 %shard_map.112 = (f32[64,128]{1,0:T(8,128)}, bf16[512,2048]{1,0:T(8,128)(2,1)}, f32[8,256]{1,0:T(8,128)}) custom-call(s32[128,32]{1,0:T(8,128)} %copy.16.ids_ref, bf16[4,2,64,128]{3,2,1,0:T(8,128)(2,1)} %bitcast.6, s32[128,2]{1,0:T(8,128)} %copy.17.route_ref, f32[128,2]{1,0:T(8,128)} %copy.18.gate_ref, f32[128,8]{1,0:T(8,128)} %copy.19.labels_ref, ...), custom_call_target="tpu_custom_call" | custom-call | tf_op jit(solution)/shard_map/pallas_call | solution.py:710
  154.1 0.0 copy-start
  154.1 0.0 copy-start.1
  154.1 4.1 %convert_element_type.3 = f32[512,2048]{1,0:T(8,128)} convert(bf16[512,2048]{1,0:T(8,128)(2,1)} %get-tuple-element.7) | non-fusion elementwise | flops 1048576 | bytes 6291456 | tf_op jit(solution)/shard_map/convert_element_type | solution.py:734
  158.2 0.0 copy-done
  158.2 0.6 copy.22
  158.9 0.0 copy-done.1
  158.9 0.6 copy.23
Async XLA Ops:
  154.1 4.2 %copy-start = (f32[64,128]{1,0:T(8,128)S(1)}, f32[64,128]{1,0:T(8,128)}, u32[]{:S(2)}) copy-start(f32[64,128]{1,0:T(8,128)} %get-tuple-element.12) | copy-start | bytes 98308
  154.1 4.8 %copy-start.1 = (f32[8,256]{1,0:T(8,128)S(1)}, f32[8,256]{1,0:T(8,128)}, u32[]{:S(2)}) copy-start(f32[8,256]{1,0:T(8,128)} %get-tuple-element.14) | copy-start | bytes 24580

commit v2 on v0

v2 whole, which is shorter than its diff:
```python
import functools
import math

import jax
import jax.numpy as jnp
from jax import lax
from jax.experimental import pallas as pl
from jax.experimental.pallas import tpu as pltpu
from jax.sharding import PartitionSpec as P

MESH = pl.DeviceIdType.MESH
F32 = jnp.float32
BF16 = jnp.bfloat16
LANES = 128
HALVES = 2
CHUNK = 256
TILE = 512


IDS, EMB_A, EMB_B, COMB, DTOW, GTO_A, GTO_B, GTO_E = range(8)
TOW_A, TOW_B, TOW_X, GIN_X, GIN_B, GIN_A, GIN_S = range(8, 15)
BACK, GRAD_A, GRAD_B, GRAD_X = range(15, 19)
DBOX = 20
PART = 24
DBACK = 28
DPOOL = 32
BOX = 36
N_SEMS = 44


def dot(a, b):
    return lax.dot_general(a, b, (((1,), (0,)), ((), ())), preferred_element_type=F32)


def dot_nt(a, b):
    return lax.dot_general(a, b, (((1,), (1,)), ((), ())), preferred_element_type=F32)


def silu_grad(pre, sig):
    return sig * (1.0 + pre * (1.0 - sig))


def kernel(
    n_table,
    n_expert,
    ids_ref,
    emb_ref,
    route_ref,
    gate_ref,
    labels_ref,
    tout_ref,
    w_in_hbm,
    w_out_hbm,
    tin_hbm,
    grows_ref,
    gin_hbm,
    gtout_ref,
    w_in,
    w_out,
    tin,
    ids,
    narrow,
    counts,
    rows,
    part_out,
    part_in,
    place,
    place_sum,
    place_t,
    place_both_t,
    outbox,
    inbox,
    acc,
    slope,
    made,
    returned,
    comb,
    dtow,
    dtow_own,
    comb_t,
    tower_a_out,
    tower_a_in,
    tower_b_out,
    tower_b_in,
    tower_x_out,
    tower_x_in,
    gin,
    gto_out,
    gto_a,
    gto_b,
    gto_e,
    dout,
    din,
    dpre,
    drows,
    dback,
    dpooled_t,
    grad_acc,
    ga_out,
    ga_in,
    gb_out,
    gb_in,
    gx_out,
    gx_in,
    local_sem,
    ss,
    rs,
):
    t = lax.axis_index("table")
    e = lax.axis_index("expert")
    n_x = n_expert // 2
    side = math.isqrt(n_table)
    x = e // 2
    core = e % 2
    sib = 1 - core
    first = core == 0
    a = jnp.where(first, t // side, t % side)
    b = jnp.where(first, t % side, t // side)
    a_step = jnp.where(first, side, 1)
    b_step = jnp.where(first, 1, side)
    lookups, batch = ids_ref.shape
    n_chunks = outbox.shape[0]
    width = n_chunks * CHUNK
    n_feat = width // LANES
    bag = lookups // n_feat
    cap = inbox.shape[2]
    slots = n_expert * cap
    hid = w_in.shape[1]
    eout = w_out.shape[1]
    tasks, tw = tout_ref.shape
    per = emb_ref.shape[2]
    span = n_x * per
    cols = n_table * span
    rel_per = n_expert // HALVES
    m_rows = rel_per * cap
    per_chunk = CHUNK // LANES

    def rel_expert(i):
        return lax.rem(x + i // 2, n_x) * 2 + lax.rem(core + i % 2, 2)

    def rel_back(i):
        return (n_x - i // 2) % n_x * 2 + i % 2

    rel_order = sorted(range(1, n_expert), key=lambda i: (min(i // 2, n_x - i // 2), -(i // 2)))

    def remote(src, dst, k_send, k_recv, to_t, to_e):
        return pltpu.make_async_remote_copy(
            src_ref=src, dst_ref=dst, send_sem=ss.at[k_send], recv_sem=rs.at[k_recv],
            device_id=(to_t, to_e), device_id_type=MESH,
        )

    def took(ref, sem):
        pltpu.make_async_copy(ref, ref, sem).wait()

    sent = []

    def to_sibling(src, dst, k):
        remote(src, dst, k, k, t, x * 2 + sib).start()
        sent.append((src, k))

    def fan_a(src, dst, k, total):
        for i in range(1, side):
            to = lax.rem(a + i, side)
            remote(src(to), dst, k, k, to * a_step + b * b_step, e).start()
        sent.append((total, k))

    def fan_b(src, dst, k, total):
        for i in range(1, side):
            to = lax.rem(b + i, side)
            remote(src(to), dst, k, k, a * a_step + to * b_step, e).start()
        sent.append((total, k))

    def fan_x(src, dst, k, total):
        for i in range(1, n_x):
            to = lax.rem(x + i, n_x)
            remote(src(to), dst, k, k, t, to * 2 + core).start()
        sent.append((total, k))

    def sum_of(ref, n):
        total = ref[0].astype(F32)
        for i in range(1, n):
            total += ref[i].astype(F32)
        return total

    w_in_copy = pltpu.make_async_copy(w_in_hbm, w_in, local_sem.at[0])
    w_out_copy = pltpu.make_async_copy(w_out_hbm, w_out, local_sem.at[1])
    tin_copy = pltpu.make_async_copy(tin_hbm, tin, local_sem.at[2])

    barrier = pltpu.get_barrier_semaphore()
    for i in range(1, side):
        for to_t in (lax.rem(a + i, side) * a_step + b * b_step, a * a_step + lax.rem(b + i, side) * b_step):
            pl.semaphore_signal(barrier, inc=1, device_id=(to_t, e), device_id_type=MESH)
    for i in range(1, n_expert):
        pl.semaphore_signal(barrier, inc=1, device_id=(t, rel_expert(i)), device_id_type=MESH)

    ids[0] = ids_ref[...]
    rows[a, b] = emb_ref[:, core].reshape(span, LANES)
    pl.semaphore_wait(barrier, 2 * (side - 1) + n_expert - 1)

    fan_a(lambda to: rows.at[a, b], rows.at[a, b], EMB_A, rows.at[0, pl.ds(0, side - 1)])
    to_sibling(ids.at[0], ids.at[1], IDS)
    w_in_copy.start()
    w_out_copy.start()
    tin_copy.start()

    narrow[...] = jnp.zeros_like(narrow)
    narrow[0:2] = route_ref[...].astype(F32)
    narrow[8:10] = gate_ref[...]
    narrow[16 : 16 + tasks] = labels_ref[...]
    columns = narrow[...].T
    lane = lax.broadcasted_iota(jnp.int32, (batch, LANES), 1)
    slot_lane = lax.broadcasted_iota(jnp.int32, (batch, slots), 1)
    r0, r1 = columns[:, 0:1].astype(jnp.int32), columns[:, 1:2].astype(jnp.int32)
    gate0, gate1 = columns[:, 8:9], columns[:, 9:10]
    named0, named1 = lane == r0, lane == r1
    named = jnp.where(named0 | named1, 1.0, 0.0).astype(BF16)
    earlier = jnp.where(
        lax.broadcasted_iota(jnp.int32, (batch, batch), 1) < lax.broadcasted_iota(jnp.int32, (batch, batch), 0),
        1.0, 0.0,
    ).astype(BF16)
    before = dot(earlier, named)
    placed = []
    for j, (r, hit) in enumerate(((r0, named0), (r1, named1))):
        pos = jnp.sum(jnp.where(hit, before, 0.0), axis=1, keepdims=True).astype(jnp.int32)
        placed.append(jnp.where(slot_lane == r * cap + pos, 1.0, 0.0))
        place[j] = placed[j].astype(BF16)
        place_both_t[:, j * batch : (j + 1) * batch] = placed[j].T.astype(BF16)
    both = placed[0] + placed[1]
    place_sum[...] = both.astype(BF16)
    place_t[...] = both.T.astype(BF16)

    def build_counts(s):
        own = ids[s]
        shard = own // (n_x * 2 * per)
        near = lax.rem(own // (2 * per), n_x) * per + lax.rem(own, per)
        at_a = jnp.where(first, shard // side, lax.rem(shard, side))
        at_b = jnp.where(first, lax.rem(shard, side), shard // side)
        code = jnp.where(lax.rem(own // per, 2) == core, (at_a * side + at_b) * span + near, -1)
        flat = jnp.concatenate([code.astype(F32), jnp.zeros((LANES - lookups, batch), F32)], axis=0)
        code = flat.T.astype(jnp.int32)
        for f in range(n_feat):
            words = [jnp.zeros((batch, LANES), jnp.int32) for _ in range(-(-cols // (8 * LANES)))]
            for k in range(bag):
                c = f * bag + k
                gap = code[:, c : c + 1] - lane
                high = gap >> 7
                one = jnp.where(jnp.bitwise_and(gap, LANES - 1) == 0, 1 << (jnp.bitwise_and(high, 7) * 4), 0)
                which = high >> 3
                for w in range(len(words)):
                    words[w] = words[w] + jnp.where(which == w, one, 0)
            for h in range(cols // LANES):
                count = jnp.bitwise_and(words[h // 8] >> (4 * (h % 8)), 15)
                counts[s, f * batch : (f + 1) * batch, h * LANES : (h + 1) * LANES] = count.astype(F32).astype(BF16)

    build_counts(0)
    took(rows.at[0, pl.ds(0, side - 1)], rs.at[EMB_A])
    fan_b(lambda to: rows.at[:, b], rows.at[:, b], EMB_B, rows.at[pl.ds(0, side - 1)])
    took(ids.at[1], rs.at[IDS])
    build_counts(1)
    took(rows.at[pl.ds(0, side - 1)], rs.at[EMB_B])

    def partial(s, c):
        return dot(counts[s, c * CHUNK : (c + 1) * CHUNK, :], rows[...].reshape(cols, LANES))

    def swap_partial(c):
        part_out[c] = partial(1, c)
        to_sibling(part_out.at[c], part_in.at[c], PART + c)

    swap_partial(0)
    for c in range(n_chunks):
        mine = partial(0, c)
        if c + 1 < n_chunks:
            swap_partial(c + 1)
        took(part_in.at[c], rs.at[PART + c])
        pooled = (mine + part_in[c]).astype(BF16)
        tokens = jnp.concatenate([pooled[f * batch : (f + 1) * batch] for f in range(per_chunk)], axis=1)
        outbox[c] = dot(place_t[...], tokens).astype(BF16).reshape(n_expert, cap, CHUNK)
        for i in rel_order:
            at = rel_back(i)
            to = rel_expert(i)
            k = BOX + c * HALVES + at // rel_per
            remote(outbox.at[c, to], inbox.at[c, at], BOX + c, k, t, to).start()
        sent.append((outbox.at[c, pl.ds(0, n_expert - 1)], BOX + c))
        inbox[c, 0] = outbox[c, e]

    w_in_copy.wait()
    w_out_copy.wait()

    def half_rels(half):
        return half * rel_per, rel_per

    def arrived(half):
        return pl.ds(max(1, half * rel_per), rel_per - (half == 0))

    for half in range(HALVES):
        for c in range(n_chunks):
            took(inbox.at[c, arrived(half)], rs.at[BOX + c * HALVES + half])
        acc[...] = jnp.zeros_like(acc)
        mine = slice(half * rel_per, (half + 1) * rel_per)

        @pl.loop(0, hid // TILE)
        def _(n):
            at = pl.ds(pl.multiple_of(n * TILE, TILE), TILE)
            block = jnp.concatenate([inbox[c, mine].reshape(m_rows, CHUNK) for c in range(n_chunks)], axis=1)
            pre = dot(block, w_in[:, at])
            sig = jax.nn.sigmoid(pre)
            slope[half, :, at] = silu_grad(pre, sig).astype(BF16)
            acc[...] += dot((pre * sig).astype(BF16), w_out[at, :])

        made[mine] = acc[...].astype(BF16).reshape(rel_per, cap, eout)
        for i in rel_order:
            if i // rel_per == half:
                remote(made.at[i], returned.at[e], BACK, BACK, t, rel_expert(i)).start()

    sent.append((made.at[pl.ds(1, n_expert - 1)], BACK))
    returned[e] = made[0]
    tin_copy.wait()
    took(returned.at[pl.ds(0, n_expert - 1)], rs.at[BACK])

    answers = returned[...].reshape(slots, eout)
    combined = (gate0 * dot(place[0], answers) + gate1 * dot(place[1], answers)).astype(BF16)
    comb[0] = combined
    dcomb = jnp.zeros((batch, eout), F32)
    per_half = tasks // 2
    for k in range(tasks):
        pre = dot(combined, tin[:, k * tw : (k + 1) * tw])
        sig = jax.nn.sigmoid(pre)
        units = pre * sig
        out_row = tout_ref[k : k + 1, :]
        logit = jnp.sum(units * out_row, axis=1, keepdims=True)
        dlogit = (jax.nn.sigmoid(logit) - columns[:, 16 + k : 17 + k]) / tasks
        gto_out[0, k : k + 1, :] = jnp.sum(dlogit * units, axis=0, keepdims=True)
        grad = (dlogit * out_row * silu_grad(pre, sig)).astype(BF16)
        dtow[k // per_half, :, (k % per_half) * tw : (k % per_half + 1) * tw] = grad
        dcomb += dot_nt(grad, tin[:, k * tw : (k + 1) * tw])
    dent = jnp.concatenate([(gate0 * dcomb).astype(BF16), (gate1 * dcomb).astype(BF16)], axis=0)
    dout[...] = dot(place_both_t[...], dent).astype(BF16).reshape(n_expert, cap, eout)
    for i in rel_order:
        at = rel_back(i)
        to = rel_expert(i)
        remote(dout.at[to], din.at[at], DBOX, DBOX + at // rel_per, t, to).start()
    sent.append((dout.at[pl.ds(0, n_expert - 1)], DBOX))
    din[0] = dout[e]

    to_sibling(comb.at[0], comb.at[1], COMB)
    to_sibling(dtow.at[sib], dtow_own.at[1], DTOW)
    fan_a(lambda to: gto_out.at[0], gto_a.at[a], GTO_A, gto_a.at[pl.ds(0, side - 1)])
    gto_a[a] = gto_out[0]
    dtow_own[0] = dtow[core]
    comb_t[:, 0:batch] = comb[0].astype(F32).T.astype(BF16)
    took(comb.at[1], rs.at[COMB])
    took(dtow_own.at[1], rs.at[DTOW])
    comb_t[:, batch : 2 * batch] = comb[1].astype(F32).T.astype(BF16)
    t_rows = eout // n_table
    t_cols = tasks * tw // 2
    x_cols = t_cols // n_x
    big = side * t_rows

    @pl.loop(0, side)
    def _(i):
        block = dot(comb_t[pl.ds(pl.multiple_of(i * big, big), big), :], dtow_own[...].reshape(2 * batch, t_cols))
        tower_a_out[i] = block.astype(BF16)

    fan_a(lambda to: tower_a_out.at[to], tower_a_in.at[a], TOW_A, tower_a_in.at[pl.ds(0, side - 1)])
    tower_a_in[a] = tower_a_out[a]

    for half in range(HALVES):
        took(din.at[arrived(half)], rs.at[DBOX + half])
        mine = slice(half * rel_per, (half + 1) * rel_per)

        @pl.loop(0, hid // TILE)
        def _(n):
            at = pl.ds(pl.multiple_of(n * TILE, TILE), TILE)
            dhid = dot_nt(din[mine].reshape(m_rows, eout), w_out[at, :])
            dpre[half, :, at] = (dhid * slope[half, :, at].astype(F32)).astype(BF16)

    took(tower_a_in.at[pl.ds(0, side - 1)], rs.at[TOW_A])
    took(gto_a.at[pl.ds(0, side - 1)], rs.at[GTO_A])
    tower_b_out[...] = sum_of(tower_a_in, side).astype(BF16).reshape(side, t_rows, t_cols)
    fan_b(lambda to: tower_b_out.at[to], tower_b_in.at[b], TOW_B, tower_b_in.at[pl.ds(0, side - 1)])
    tower_b_in[b] = tower_b_out[b]
    gto_out[1] = sum_of(gto_a, side)
    fan_b(lambda to: gto_out.at[1], gto_b.at[b], GTO_B, gto_b.at[pl.ds(0, side - 1)])
    gto_b[b] = gto_out[1]

    def token_grads(c):
        for half in range(HALVES):
            block = dot_nt(dpre[half], w_in[c * CHUNK : (c + 1) * CHUNK, :])
            drows[c, half * rel_per : (half + 1) * rel_per] = block.astype(BF16).reshape(rel_per, cap, CHUNK)
        for i in rel_order:
            remote(drows.at[c, i], dback.at[c, e], DBACK + c, DBACK + c, t, rel_expert(i)).start()
        sent.append((drows.at[c, pl.ds(1, n_expert - 1)], DBACK + c))
        dback[c, e] = drows[c, 0]

    def pooled_grads(c):
        took(dback.at[c, pl.ds(0, n_expert - 1)], rs.at[DBACK + c])
        got = dot(place_sum[...], dback[c].reshape(slots, CHUNK)).astype(BF16).astype(F32)
        for f in range(per_chunk):
            dpooled_t[c, 0, :, f * batch : (f + 1) * batch] = got[:, f * LANES : (f + 1) * LANES].T.astype(BF16)
        to_sibling(dpooled_t.at[c, 0], dpooled_t.at[c, 1], DPOOL + c)

    big_cols = side * span

    def row_grads(c, at_a):
        at = pl.ds(pl.multiple_of(at_a * big_cols, big_cols), big_cols)
        total = dot(dpooled_t[c, 0], counts[0, c * CHUNK : (c + 1) * CHUNK, at])
        total += dot(dpooled_t[c, 1], counts[1, c * CHUNK : (c + 1) * CHUNK, at])
        return total if c == 0 else total + grad_acc[at_a]

    def add_chunk(c):
        took(dpooled_t.at[c, 1], rs.at[DPOOL + c])

        @pl.loop(0, side)
        def _(at_a):
            grad_acc[at_a] = row_grads(c, at_a)

    def gin_rows(at, n):
        return pl.ds(pl.multiple_of(at * t_rows, t_rows), n * t_rows)

    my_rows, my_big = gin_rows(a * side + b, 1), gin_rows(a * side, side)
    x_at = pl.ds(pl.multiple_of(x * x_cols, x_cols), x_cols)

    def tower_second():
        took(tower_b_in.at[pl.ds(0, side - 1)], rs.at[TOW_B])
        took(gto_b.at[pl.ds(0, side - 1)], rs.at[GTO_B])
        total = sum_of(tower_b_in, side)
        for k in range(n_x):
            tower_x_out[k] = total[:, k * x_cols : (k + 1) * x_cols].astype(BF16)
        fan_x(lambda to: tower_x_out.at[to], tower_x_in.at[x], TOW_X, tower_x_in.at[pl.ds(0, n_x - 1)])
        tower_x_in[x] = tower_x_out[x]
        gto_out[2] = sum_of(gto_b, side)
        for i in rel_order:
            remote(gto_out.at[2], gto_e.at[e], GTO_E, GTO_E, t, rel_expert(i)).start()
        sent.append((gto_e.at[pl.ds(0, n_expert - 1)], GTO_E))
        gto_e[e] = gto_out[2]

    def tower_x():
        took(tower_x_in.at[pl.ds(0, n_x - 1)], rs.at[TOW_X])
        gin[core, my_rows, x_at] = sum_of(tower_x_in, n_x).astype(BF16)
        block = gin.at[core, my_rows, x_at]
        fan_x(lambda to: block, block, GIN_X, tower_x_in.at[pl.ds(0, n_x - 1)])

    def gather_x():
        took(tower_x_in.at[pl.ds(0, n_x - 1)], rs.at[GIN_X])
        block = gin.at[core, my_rows]
        fan_b(lambda to: block, block, GIN_B, tower_b_in.at[pl.ds(0, side - 1)])

    def gather_b():
        took(tower_b_in.at[pl.ds(0, side - 1)], rs.at[GIN_B])
        block = gin.at[core, my_big]
        fan_a(lambda to: block, block, GIN_A, tower_a_in.at[pl.ds(0, side - 1)])

    beside = {1: tower_second, 3: tower_x}
    for c in range(n_chunks):
        token_grads(c)
        if c in beside:
            beside[c]()
    beside = {1: gather_x, 2: gather_b}
    for c in range(n_chunks):
        pooled_grads(c)
        if c > 0:
            add_chunk(c - 1)
        if c in beside:
            beside[c]()

    last = n_chunks - 1
    took(dpooled_t.at[last, 1], rs.at[DPOOL + last])
    for i in range(1, side):
        to = lax.rem(a + i, side)
        ga_out[to] = row_grads(last, to).astype(BF16)
        remote(ga_out.at[to], ga_in.at[a], GRAD_A, GRAD_A, to * a_step + b * b_step, e).start()
    sent.append((ga_in.at[pl.ds(0, side - 1)], GRAD_A))
    ga_in[a] = row_grads(last, a).astype(BF16)

    took(tower_a_in.at[pl.ds(0, side - 1)], rs.at[GIN_A])
    to_sibling(gin.at[core], gin.at[core], GIN_S)
    took(gto_e.at[pl.ds(0, n_expert - 1)], rs.at[GTO_E])
    gtout_ref[...] = sum_of(gto_e, n_expert)
    took(gin.at[0], rs.at[GIN_S])
    gin_outs = [
        pltpu.make_async_copy(gin.at[h], gin_hbm.at[:, pl.ds(h * t_cols, t_cols)], local_sem.at[3 + h]) for h in range(2)
    ]
    for copy in gin_outs:
        copy.start()

    took(ga_in.at[pl.ds(0, side - 1)], rs.at[GRAD_A])
    total = sum_of(ga_in, side)
    for k in range(side):
        gb_out[k] = total[:, k * span : (k + 1) * span].astype(BF16)
    fan_b(lambda to: gb_out.at[to], gb_in.at[b], GRAD_B, gb_in.at[pl.ds(0, side - 1)])
    gb_in[b] = gb_out[b]
    took(gb_in.at[pl.ds(0, side - 1)], rs.at[GRAD_B])
    gx_out[...] = sum_of(gb_in, side).T.astype(BF16).reshape(n_x, per, LANES)
    fan_x(lambda to: gx_out.at[to], gx_in.at[x], GRAD_X, gx_in.at[pl.ds(0, n_x - 1)])
    gx_in[x] = gx_out[x]
    took(gx_in.at[pl.ds(0, n_x - 1)], rs.at[GRAD_X])
    grows_ref[...] = sum_of(gx_in, n_x)

    for ref, k in sent:
        took(ref, ss.at[k])
    for copy in gin_outs:
        copy.wait()


def finish(gin_ref, grows_ref, gto_ref, gin_out, grows_out, gto_out):
    gin_out[...] = gin_ref[...].astype(F32)
    grows_out[...] = grows_ref[...]
    gto_out[...] = gto_ref[...]


def per_device(emb_rows, row_ids, route_ids, route_gates, w_in, w_out, tower_in, tower_out, labels):
    n_table = lax.axis_size("table")
    n_expert = lax.axis_size("expert")
    n_x = n_expert // 2
    side = math.isqrt(n_table)
    samples, tables, bag = row_ids.shape
    cap = 3 * samples // n_expert
    row_dev, dim = emb_rows.shape
    width = tables * dim
    hid, eout = w_out.shape[1:]
    tasks, tw = tower_out.shape
    per = row_dev // n_expert
    span = n_x * per
    cols = n_table * span
    slots = n_expert * cap
    n_chunks = width // CHUNK
    m_rows = slots // HALVES
    t_rows = eout // n_table
    t_cols = tasks * tw // 2
    x_cols = t_cols // n_x
    vmem = pl.BlockSpec(memory_space=pltpu.VMEM)
    hbm = pl.BlockSpec(memory_space=pl.ANY)
    dma = pltpu.SemaphoreType.DMA
    scratch = [
        pltpu.VMEM((width, hid), BF16),
        pltpu.VMEM((hid, eout), BF16),
        pltpu.VMEM((eout, tasks * tw), BF16),
        pltpu.VMEM((2, tables * bag, samples), jnp.int32),
        pltpu.VMEM((LANES, samples), F32),
        pltpu.VMEM((2, width, cols), BF16),
        pltpu.VMEM((side, side, span, LANES), BF16),
        pltpu.VMEM((n_chunks, CHUNK, LANES), F32),
        pltpu.VMEM((n_chunks, CHUNK, LANES), F32),
        pltpu.VMEM((2, samples, slots), BF16),
        pltpu.VMEM((samples, slots), BF16),
        pltpu.VMEM((slots, samples), BF16),
        pltpu.VMEM((slots, 2 * samples), BF16),
        pltpu.VMEM((n_chunks, n_expert, cap, CHUNK), BF16),
        pltpu.VMEM((n_chunks, n_expert, cap, CHUNK), BF16),
        pltpu.VMEM((m_rows, eout), F32),
        pltpu.VMEM((HALVES, m_rows, hid), BF16),
        pltpu.VMEM((n_expert, cap, eout), BF16),
        pltpu.VMEM((n_expert, cap, eout), BF16),
        pltpu.VMEM((2, samples, eout), BF16),
        pltpu.VMEM((2, samples, t_cols), BF16),
        pltpu.VMEM((2, samples, t_cols), BF16),
        pltpu.VMEM((eout, 2 * samples), BF16),
        pltpu.VMEM((side, side * t_rows, t_cols), BF16),
        pltpu.VMEM((side, side * t_rows, t_cols), BF16),
        pltpu.VMEM((side, t_rows, t_cols), BF16),
        pltpu.VMEM((side, t_rows, t_cols), BF16),
        pltpu.VMEM((n_x, t_rows, x_cols), BF16),
        pltpu.VMEM((n_x, t_rows, x_cols), BF16),
        pltpu.VMEM((2, eout, t_cols), BF16),
        pltpu.VMEM((3, tasks, tw), F32),
        pltpu.VMEM((side, tasks, tw), F32),
        pltpu.VMEM((side, tasks, tw), F32),
        pltpu.VMEM((n_expert, tasks, tw), F32),
        pltpu.VMEM((n_expert, cap, eout), BF16),
        pltpu.VMEM((n_expert, cap, eout), BF16),
        pltpu.VMEM((HALVES, m_rows, hid), BF16),
        pltpu.VMEM((n_chunks, n_expert, cap, CHUNK), BF16),
        pltpu.VMEM((n_chunks, n_expert, cap, CHUNK), BF16),
        pltpu.VMEM((n_chunks, 2, LANES, CHUNK), BF16),
        pltpu.VMEM((side, LANES, side * span), F32),
        pltpu.VMEM((side, LANES, side * span), BF16),
        pltpu.VMEM((side, LANES, side * span), BF16),
        pltpu.VMEM((side, LANES, span), BF16),
        pltpu.VMEM((side, LANES, span), BF16),
        pltpu.VMEM((n_x, per, LANES), BF16),
        pltpu.VMEM((n_x, per, LANES), BF16),
        dma((5,)),
        dma((N_SEMS,)),
        dma((N_SEMS,)),
    ]
    grows, gin, gtout = pl.pallas_call(
        functools.partial(kernel, n_table, n_expert),
        out_shape=(
            jax.ShapeDtypeStruct((per, dim), F32),
            jax.ShapeDtypeStruct((eout, tasks * tw), BF16),
            jax.ShapeDtypeStruct((tasks, tw), F32),
        ),
        in_specs=[vmem] * 6 + [hbm] * 3,
        out_specs=(vmem, hbm, vmem),
        scratch_shapes=scratch,
        compiler_params=pltpu.CompilerParams(
            collective_id=0, has_side_effects=True, vmem_limit_bytes=VMEM_LIMIT
        ),
    )(
        jnp.transpose(row_ids, (1, 2, 0)).reshape(tables * bag, samples),
        emb_rows.reshape(n_x, 2, per, dim),
        route_ids.T,
        route_gates.T,
        labels.T,
        tower_out,
        w_in[0],
        w_out[0],
        tower_in,
    )
    whole = lambda shape: pl.BlockSpec(shape, lambda i: (0, 0))
    piece = pl.BlockSpec((eout // 4, tasks * tw), lambda i: (i, 0))
    gin, grows, gtout = pl.pallas_call(
        finish,
        grid=(4,),
        out_shape=(
            jax.ShapeDtypeStruct((eout, tasks * tw), F32),
            jax.ShapeDtypeStruct((per, dim), F32),
            jax.ShapeDtypeStruct((tasks, tw), F32),
        ),
        in_specs=[piece, whole((per, dim)), whole((tasks, tw))],
        out_specs=(piece, whole((per, dim)), whole((tasks, tw))),
    )(gin, grows, gtout)
    return grows, gin, gtout


VMEM_LIMIT = 63 * 1024 * 1024


def solution(mesh):
    return jax.shard_map(
        per_device,
        mesh=mesh,
        in_specs=(
            P("table", None),
            P(("table", "expert"), None, None),
            P(("table", "expert"), None),
            P(("table", "expert"), None),
            P("expert", None, None),
            P("expert", None, None),
            P(),
            P(),
            P(("table", "expert"), None),
        ),
        out_specs=(P(("table", "expert"), None), P(), P()),
        check_vma=False,
    )
```

time: 561 us -> 114 us (0.20)
  waiting for transfers between devices: 265 us -> 0 us
  blocking collectives: 136 us -> 0 us
  Pallas kernels: 0 us -> 113 us
  matrix products: 71.2 us -> 0 us
  other arithmetic: 58.1 us -> 0 us
  between operations: 14 us -> 0.64 us
  local copies, waits for them, and re-layouts: 11.7 us -> 0 us
    psum x1 -> x0, waiting for transfers between devices: 119 us -> none  [per_device(): lax.psum((local_in, local_out), ('table', 'expert'))]
    pallas_call x0 -> x2, Pallas kernels: none -> 113 us  [the longest x1 109 us: per_device(): pl.pallas_call(functools.partial(kernel, n_table, n_expert), out_shape=(j...]
    reduce_scatter x2 -> x0, waiting for transfers between devices: 82.3 us -> none  [the longest x1 82.2 us: per_device(): lax.psum_scatter(pool_owned(emb_rows, all_ids, shard * row_dev), 'table',...]
    dot_general x27 -> x0, matrix products: 71.2 us -> none  [the longest x8 21.9 us: one_table(): return jnp.dot(counts, table_rows, preferred_element_type=jnp.float32)]
    psum x1 -> x0, blocking collectives: 64.6 us -> none  [per_device(): lax.psum((local_in, local_out), ('table', 'expert'))]
    all_gather x1 -> x0, waiting for transfers between devices: 55.2 us -> none  [per_device(): group_grads = lax.all_gather(dpooled, 'table', axis=0, tiled=True)]
    reduce_sum x19 -> x0, other arithmetic: 52.5 us -> none  [the longest x16 52.1 us: bag_counts(): return jnp.sum(hits, axis=1).astype(jnp.bfloat16)]
    all_to_all x3 -> x0, blocking collectives: 45.4 us -> none  [move_slots(): lax.all_to_all(boxes, 'expert', split_axis=0, concat_axis=0, tiled=True)]
  transfers between devices with their start and end apart: 5 -> 0, of which waited for: 4 -> 0; matrix products, arithmetic and copies ran while one was open for 1% -> 0% of each run, Pallas kernels for 0% -> 0%
where the time goes in v2:
time: 114 us
  Pallas kernels  113 us (99%)
    pallas_call x1, Pallas kernels, per_device(): pl.pallas_call(functools.partial(kernel, n_table, n_expert), out_shape=(j...  109 us
    pallas_call x1, Pallas kernels, per_device(): pl.pallas_call(finish, grid=(4,), out_shape=(jax.ShapeDtypeStruct((eout,...  4.22 us

profile of v2, /device:TPU:0, one launch (start us, length us, event | category | flops | bytes accessed | tf_op | source)
XLA Modules:
  0.0 114.1 jit_solution(7995420046756304021)
XLA Ops:
  0.6 109.3 %shard_map.112 = (f32[64,128]{1,0:T(8,128)}, bf16[512,2048]{1,0:T(8,128)(2,1)}, f32[8,256]{1,0:T(8,128)}) custom-call(s32[32,128]{1,0:T(8,128)} %bitcast.12, bf16[4,2,64,128]{3,2,1,0:T(8,128)(2,1)} %bitcast.11, s32[2,128]{1,0:T(2,128)} %bitcast.14, f32[2,128]{1,0:T(2,128)} %bitcast.15, f32[8,128]{1,0:T(8,128)} %bitcast.13, f32[8,256]{1,0:T(8,128)} %tout_ref.1, ...), custom_call_target="tpu_custom_call" | custom-call | tf_op jit(solution)/shard_map/pallas_call | solution.py:586
  109.9 4.2 %shard_map.113 = (f32[512,2048]{1,0:T(8,128)}, f32[64,128]{1,0:T(8,128)}, f32[8,256]{1,0:T(8,128)}) custom-call(bf16[512,2048]{1,0:T(8,128)(2,1)} %get-tuple-element.9.gin_ref, f32[64,128]{1,0:T(8,128)} %get-tuple-element.10.grows_ref, f32[8,256]{1,0:T(8,128)} %get-tuple-element.11.gto_ref), custom_call_target="tpu_custom_call" | custom-call | tf_op jit(solution)/shard_map/pallas_call | solution.py:612

commit v3 on v2

--- a/solution.py
+++ b/solution.py
@@ -14,18 +14,18 @@
 LANES = 128
 HALVES = 2
 CHUNK = 256
-TILE = 512
+TILE = 2048
 
 
 IDS, EMB_A, EMB_B, COMB, DTOW, GTO_A, GTO_B, GTO_E = range(8)
-TOW_A, TOW_B, TOW_X, GIN_X, GIN_B, GIN_A, GIN_S = range(8, 15)
+TOW_A, TOW_B, TOW_X, GIN_B, GIN_A, GIN_S = range(8, 14)
 BACK, GRAD_A, GRAD_B, GRAD_X = range(15, 19)
 DBOX = 20
 PART = 24
 DBACK = 28
 DPOOL = 32
 BOX = 36
-N_SEMS = 44
+N_SEMS = 40
 
 
 def dot(a, b):
@@ -63,6 +63,7 @@
     counts,
     rows,
     part_out,
+    part_own,
     part_in,
     place,
     place_sum,
@@ -71,6 +72,7 @@
     outbox,
     inbox,
     acc,
+    pre_acc,
     slope,
     made,
     returned,
@@ -91,7 +93,6 @@
     gto_e,
     dout,
     din,
-    dpre,
     drows,
     dback,
     dpooled_t,
@@ -135,13 +136,21 @@
     m_rows = rel_per * cap
     per_chunk = CHUNK // LANES
 
+    far = n_x // 2
+    rels = [(far, 0), (far, 1)]
+    rels += [(d, 0) for d in range(1, n_x) if d != far]
+    rels += [(0, 0), (0, 1)]
+    rels += [(d, 1) for d in range(1, n_x) if d != far]
+    me = rels.index((0, 0))
+    others = [i for i in range(n_expert) if i != me]
+
     def rel_expert(i):
-        return lax.rem(x + i // 2, n_x) * 2 + lax.rem(core + i % 2, 2)
+        d, c = rels[i]
+        return lax.rem(x + d, n_x) * 2 + lax.rem(core + c, 2)
 
     def rel_back(i):
-        return (n_x - i // 2) % n_x * 2 + i % 2
-
-    rel_order = sorted(range(1, n_expert), key=lambda i: (min(i // 2, n_x - i // 2), -(i // 2)))
+        d, c = rels[i]
+        return rels.index(((n_x - d) % n_x, c))
 
     def remote(src, dst, k_send, k_recv, to_t, to_e):
         return pltpu.make_async_remote_copy(
@@ -190,14 +199,14 @@
     for i in range(1, side):
         for to_t in (lax.rem(a + i, side) * a_step + b * b_step, a * a_step + lax.rem(b + i, side) * b_step):
             pl.semaphore_signal(barrier, inc=1, device_id=(to_t, e), device_id_type=MESH)
-    for i in range(1, n_expert):
+    for i in others:
         pl.semaphore_signal(barrier, inc=1, device_id=(t, rel_expert(i)), device_id_type=MESH)
 
     ids[0] = ids_ref[...]
-    rows[a, b] = emb_ref[:, core].reshape(span, LANES)
+    rows[b, a] = emb_ref[:, core].reshape(span, LANES)
     pl.semaphore_wait(barrier, 2 * (side - 1) + n_expert - 1)
 
-    fan_a(lambda to: rows.at[a, b], rows.at[a, b], EMB_A, rows.at[0, pl.ds(0, side - 1)])
+    fan_a(lambda to: rows.at[b, a], rows.at[b, a], EMB_A, rows.at[0, pl.ds(0, side - 1)])
     to_sibling(ids.at[0], ids.at[1], IDS)
     w_in_copy.start()
     w_out_copy.start()
@@ -229,16 +238,18 @@
     place_sum[...] = both.astype(BF16)
     place_t[...] = both.T.astype(BF16)
 
-    def build_counts(s):
+    def code_of(s):
         own = ids[s]
         shard = own // (n_x * 2 * per)
         near = lax.rem(own // (2 * per), n_x) * per + lax.rem(own, per)
         at_a = jnp.where(first, shard // side, lax.rem(shard, side))
         at_b = jnp.where(first, lax.rem(shard, side), shard // side)
-        code = jnp.where(lax.rem(own // per, 2) == core, (at_a * side + at_b) * span + near, -1)
+        code = jnp.where(lax.rem(own // per, 2) == core, (at_b * side + at_a) * span + near, -1)
         flat = jnp.concatenate([code.astype(F32), jnp.zeros((LANES - lookups, batch), F32)], axis=0)
-        code = flat.T.astype(jnp.int32)
-        for f in range(n_feat):
+        return flat.T.astype(jnp.int32)
+
+    def build_counts(s, code, features):
+        for f in features:
             words = [jnp.zeros((batch, LANES), jnp.int32) for _ in range(-(-cols // (8 * LANES)))]
             for k in range(bag):
                 c = f * bag + k
@@ -252,75 +263,94 @@
                 count = jnp.bitwise_and(words[h // 8] >> (4 * (h % 8)), 15)
                 counts[s, f * batch : (f + 1) * batch, h * LANES : (h + 1) * LANES] = count.astype(F32).astype(BF16)
 
-    build_counts(0)
+    code = code_of(0)
+    build_counts(0, code, range(n_feat // 2))
     took(rows.at[0, pl.ds(0, side - 1)], rs.at[EMB_A])
-    fan_b(lambda to: rows.at[:, b], rows.at[:, b], EMB_B, rows.at[pl.ds(0, side - 1)])
+    fan_b(lambda to: rows.at[b], rows.at[b], EMB_B, rows.at[pl.ds(0, side - 1)])
+    build_counts(0, code, range(n_feat // 2, n_feat))
     took(ids.at[1], rs.at[IDS])
-    build_counts(1)
+    build_counts(1, code_of(1), range(n_feat))
+
+    part_cols = side * span
+
+    def partial(s, c, at_b):
+        at = pl.ds(pl.multiple_of(at_b * part_cols, part_cols), part_cols)
+        return dot(counts[s, c * CHUNK : (c + 1) * CHUNK, at], rows[at_b].reshape(part_cols, LANES))
+
+    for c in range(n_chunks):
+        part_out[c] = partial(1, c, b)
+        part_own[c] = partial(0, c, b)
     took(rows.at[pl.ds(0, side - 1)], rs.at[EMB_B])
 
-    def partial(s, c):
-        return dot(counts[s, c * CHUNK : (c + 1) * CHUNK, :], rows[...].reshape(cols, LANES))
+    def all_parts(s, c, total):
+        for i in range(1, side):
+            total += partial(s, c, lax.rem(b + i, side))
+        return total
 
     def swap_partial(c):
-        part_out[c] = partial(1, c)
+        part_out[c] = all_parts(1, c, part_out[c])
         to_sibling(part_out.at[c], part_in.at[c], PART + c)
 
     swap_partial(0)
     for c in range(n_chunks):
-        mine = partial(0, c)
+        mine = all_parts(0, c, part_own[c])
         if c + 1 < n_chunks:
             swap_partial(c + 1)
         took(part_in.at[c], rs.at[PART + c])
         pooled = (mine + part_in[c]).astype(BF16)
         tokens = jnp.concatenate([pooled[f * batch : (f + 1) * batch] for f in range(per_chunk)], axis=1)
         outbox[c] = dot(place_t[...], tokens).astype(BF16).reshape(n_expert, cap, CHUNK)
-        for i in rel_order:
-            at = rel_back(i)
+        for i in others:
             to = rel_expert(i)
-            k = BOX + c * HALVES + at // rel_per
-            remote(outbox.at[c, to], inbox.at[c, at], BOX + c, k, t, to).start()
+            remote(outbox.at[c, to], inbox.at[c, rel_back(i)], BOX + c, BOX + c, t, to).start()
         sent.append((outbox.at[c, pl.ds(0, n_expert - 1)], BOX + c))
-        inbox[c, 0] = outbox[c, e]
+        inbox[c, me] = outbox[c, e]
 
     w_in_copy.wait()
     w_out_copy.wait()
 
-    def half_rels(half):
-        return half * rel_per, rel_per
-
     def arrived(half):
-        return pl.ds(max(1, half * rel_per), rel_per - (half == 0))
-
+        return pl.ds(half * rel_per, rel_per - (me // rel_per == half))
+
+    tile = min(TILE, hid)
+
+    for c in range(n_chunks - 1):
+        took(inbox.at[c, pl.ds(0, n_expert - 1)], rs.at[BOX + c])
+
+        @pl.loop(0, hid // tile)
+        def _(n):
+            at = pl.ds(pl.multiple_of(n * tile, tile), tile)
+            pre = dot(inbox[c].reshape(slots, CHUNK), w_in[c * CHUNK : (c + 1) * CHUNK, at])
+            pre_acc[:, at] = pre if c == 0 else pre_acc[:, at] + pre
+
+    last = n_chunks - 1
+    took(inbox.at[last, pl.ds(0, n_expert - 1)], rs.at[BOX + last])
     for half in range(HALVES):
-        for c in range(n_chunks):
-            took(inbox.at[c, arrived(half)], rs.at[BOX + c * HALVES + half])
         acc[...] = jnp.zeros_like(acc)
         mine = slice(half * rel_per, (half + 1) * rel_per)
 
-        @pl.loop(0, hid // TILE)
+        @pl.loop(0, hid // tile)
         def _(n):
-            at = pl.ds(pl.multiple_of(n * TILE, TILE), TILE)
-            block = jnp.concatenate([inbox[c, mine].reshape(m_rows, CHUNK) for c in range(n_chunks)], axis=1)
-            pre = dot(block, w_in[:, at])
+            at = pl.ds(pl.multiple_of(n * tile, tile), tile)
+            pre = dot(inbox[last, mine].reshape(m_rows, CHUNK), w_in[last * CHUNK : (last + 1) * CHUNK, at])
+            pre += pre_acc[half * m_rows : (half + 1) * m_rows, at]
             sig = jax.nn.sigmoid(pre)
             slope[half, :, at] = silu_grad(pre, sig).astype(BF16)
             acc[...] += dot((pre * sig).astype(BF16), w_out[at, :])
 
         made[mine] = acc[...].astype(BF16).reshape(rel_per, cap, eout)
-        for i in rel_order:
+        for i in others:
             if i // rel_per == half:
                 remote(made.at[i], returned.at[e], BACK, BACK, t, rel_expert(i)).start()
 
-    sent.append((made.at[pl.ds(1, n_expert - 1)], BACK))
-    returned[e] = made[0]
+    sent.append((made.at[pl.ds(0, n_expert - 1)], BACK))
+    returned[e] = made[me]
     tin_copy.wait()
     took(returned.at[pl.ds(0, n_expert - 1)], rs.at[BACK])
 
     answers = returned[...].reshape(slots, eout)
     combined = (gate0 * dot(place[0], answers) + gate1 * dot(place[1], answers)).astype(BF16)
     comb[0] = combined
-    dcomb = jnp.zeros((batch, eout), F32)
     per_half = tasks // 2
     for k in range(tasks):
         pre = dot(combined, tin[:, k * tw : (k + 1) * tw])
@@ -332,18 +362,18 @@
         gto_out[0, k : k + 1, :] = jnp.sum(dlogit * units, axis=0, keepdims=True)
         grad = (dlogit * out_row * silu_grad(pre, sig)).astype(BF16)
         dtow[k // per_half, :, (k % per_half) * tw : (k % per_half + 1) * tw] = grad
-        dcomb += dot_nt(grad, tin[:, k * tw : (k + 1) * tw])
+    to_sibling(comb.at[0], comb.at[1], COMB)
+    to_sibling(dtow.at[sib], dtow_own.at[1], DTOW)
+    dcomb = sum(dot_nt(dtow[h], tin[:, h * per_half * tw : (h + 1) * per_half * tw]) for h in range(2))
     dent = jnp.concatenate([(gate0 * dcomb).astype(BF16), (gate1 * dcomb).astype(BF16)], axis=0)
     dout[...] = dot(place_both_t[...], dent).astype(BF16).reshape(n_expert, cap, eout)
-    for i in rel_order:
+    for i in reversed(others):
         at = rel_back(i)
         to = rel_expert(i)
         remote(dout.at[to], din.at[at], DBOX, DBOX + at // rel_per, t, to).start()
     sent.append((dout.at[pl.ds(0, n_expert - 1)], DBOX))
-    din[0] = dout[e]
-
-    to_sibling(comb.at[0], comb.at[1], COMB)
-    to_sibling(dtow.at[sib], dtow_own.at[1], DTOW)
+    din[me] = dout[e]
+
     fan_a(lambda to: gto_out.at[0], gto_a.at[a], GTO_A, gto_a.at[pl.ds(0, side - 1)])
     gto_a[a] = gto_out[0]
     dtow_own[0] = dtow[core]
@@ -353,7 +383,6 @@
     comb_t[:, batch : 2 * batch] = comb[1].astype(F32).T.astype(BF16)
     t_rows = eout // n_table
     t_cols = tasks * tw // 2
-    x_cols = t_cols // n_x
     big = side * t_rows
 
     @pl.loop(0, side)
@@ -364,33 +393,36 @@
     fan_a(lambda to: tower_a_out.at[to], tower_a_in.at[a], TOW_A, tower_a_in.at[pl.ds(0, side - 1)])
     tower_a_in[a] = tower_a_out[a]
 
-    for half in range(HALVES):
+    def tower_first():
+        took(tower_a_in.at[pl.ds(0, side - 1)], rs.at[TOW_A])
+        took(gto_a.at[pl.ds(0, side - 1)], rs.at[GTO_A])
+        tower_b_out[...] = sum_of(tower_a_in, side).astype(BF16).reshape(side, t_rows, t_cols)
+        fan_b(lambda to: tower_b_out.at[to], tower_b_in.at[b], TOW_B, tower_b_in.at[pl.ds(0, side - 1)])
+        tower_b_in[b] = tower_b_out[b]
+        gto_out[1] = sum_of(gto_a, side)
+        fan_b(lambda to: gto_out.at[1], gto_b.at[b], GTO_B, gto_b.at[pl.ds(0, side - 1)])
+        gto_b[b] = gto_out[1]
+
+    for half in reversed(range(HALVES)):
         took(din.at[arrived(half)], rs.at[DBOX + half])
+        if half == 0:
+            tower_first()
         mine = slice(half * rel_per, (half + 1) * rel_per)
 
-        @pl.loop(0, hid // TILE)
+        @pl.loop(0, hid // tile)
         def _(n):
-            at = pl.ds(pl.multiple_of(n * TILE, TILE), TILE)
+            at = pl.ds(pl.multiple_of(n * tile, tile), tile)
             dhid = dot_nt(din[mine].reshape(m_rows, eout), w_out[at, :])
-            dpre[half, :, at] = (dhid * slope[half, :, at].astype(F32)).astype(BF16)
-
-    took(tower_a_in.at[pl.ds(0, side - 1)], rs.at[TOW_A])
-    took(gto_a.at[pl.ds(0, side - 1)], rs.at[GTO_A])
-    tower_b_out[...] = sum_of(tower_a_in, side).astype(BF16).reshape(side, t_rows, t_cols)
-    fan_b(lambda to: tower_b_out.at[to], tower_b_in.at[b], TOW_B, tower_b_in.at[pl.ds(0, side - 1)])
-    tower_b_in[b] = tower_b_out[b]
-    gto_out[1] = sum_of(gto_a, side)
-    fan_b(lambda to: gto_out.at[1], gto_b.at[b], GTO_B, gto_b.at[pl.ds(0, side - 1)])
-    gto_b[b] = gto_out[1]
+            slope[half, :, at] = (dhid * slope[half, :, at].astype(F32)).astype(BF16)
 
     def token_grads(c):
         for half in range(HALVES):
-            block = dot_nt(dpre[half], w_in[c * CHUNK : (c + 1) * CHUNK, :])
+            block = dot_nt(slope[half], w_in[c * CHUNK : (c + 1) * CHUNK, :])
             drows[c, half * rel_per : (half + 1) * rel_per] = block.astype(BF16).reshape(rel_per, cap, CHUNK)
-        for i in rel_order:
+        for i in others:
             remote(drows.at[c, i], dback.at[c, e], DBACK + c, DBACK + c, t, rel_expert(i)).start()
-        sent.append((drows.at[c, pl.ds(1, n_expert - 1)], DBACK + c))
-        dback[c, e] = drows[c, 0]
+        sent.append((drows.at[c, pl.ds(0, n_expert - 1)], DBACK + c))
+        dback[c, e] = drows[c, me]
 
     def pooled_grads(c):
         took(dback.at[c, pl.ds(0, n_expert - 1)], rs.at[DBACK + c])
@@ -399,49 +431,42 @@
             dpooled_t[c, 0, :, f * batch : (f + 1) * batch] = got[:, f * LANES : (f + 1) * LANES].T.astype(BF16)
         to_sibling(dpooled_t.at[c, 0], dpooled_t.at[c, 1], DPOOL + c)
 
-    big_cols = side * span
-
     def row_grads(c, at_a):
-        at = pl.ds(pl.multiple_of(at_a * big_cols, big_cols), big_cols)
-        total = dot(dpooled_t[c, 0], counts[0, c * CHUNK : (c + 1) * CHUNK, at])
-        total += dot(dpooled_t[c, 1], counts[1, c * CHUNK : (c + 1) * CHUNK, at])
+        total = None
+        for s in range(2):
+            parts = [
+                counts[s, c * CHUNK : (c + 1) * CHUNK, pl.ds(pl.multiple_of((bb * side + at_a) * span, span), span)]
+                for bb in range(side)
+            ]
+            term = dot(dpooled_t[c, s], jnp.concatenate(parts, axis=1))
+            total = term if total is None else total + term
         return total if c == 0 else total + grad_acc[at_a]
 
     def add_chunk(c):
         took(dpooled_t.at[c, 1], rs.at[DPOOL + c])
-
-        @pl.loop(0, side)
-        def _(at_a):
+        for at_a in range(side):
             grad_acc[at_a] = row_grads(c, at_a)
 
     def gin_rows(at, n):
         return pl.ds(pl.multiple_of(at * t_rows, t_rows), n * t_rows)
 
     my_rows, my_big = gin_rows(a * side + b, 1), gin_rows(a * side, side)
-    x_at = pl.ds(pl.multiple_of(x * x_cols, x_cols), x_cols)
 
     def tower_second():
         took(tower_b_in.at[pl.ds(0, side - 1)], rs.at[TOW_B])
         took(gto_b.at[pl.ds(0, side - 1)], rs.at[GTO_B])
-        total = sum_of(tower_b_in, side)
-        for k in range(n_x):
-            tower_x_out[k] = total[:, k * x_cols : (k + 1) * x_cols].astype(BF16)
-        fan_x(lambda to: tower_x_out.at[to], tower_x_in.at[x], TOW_X, tower_x_in.at[pl.ds(0, n_x - 1)])
-        tower_x_in[x] = tower_x_out[x]
+        tower_x_out[...] = sum_of(tower_b_in, side).astype(BF16)
+        fan_x(lambda to: tower_x_out, tower_x_in.at[x], TOW_X, tower_x_in.at[pl.ds(0, n_x - 1)])
+        tower_x_in[x] = tower_x_out[...]
         gto_out[2] = sum_of(gto_b, side)
-        for i in rel_order:
+        for i in others:
             remote(gto_out.at[2], gto_e.at[e], GTO_E, GTO_E, t, rel_expert(i)).start()
         sent.append((gto_e.at[pl.ds(0, n_expert - 1)], GTO_E))
         gto_e[e] = gto_out[2]
 
     def tower_x():
         took(tower_x_in.at[pl.ds(0, n_x - 1)], rs.at[TOW_X])
-        gin[core, my_rows, x_at] = sum_of(tower_x_in, n_x).astype(BF16)
-        block = gin.at[core, my_rows, x_at]
-        fan_x(lambda to: block, block, GIN_X, tower_x_in.at[pl.ds(0, n_x - 1)])
-
-    def gather_x():
-        took(tower_x_in.at[pl.ds(0, n_x - 1)], rs.at[GIN_X])
+        gin[core, my_rows] = sum_of(tower_x_in, n_x).astype(BF16)
         block = gin.at[core, my_rows]
         fan_b(lambda to: block, block, GIN_B, tower_b_in.at[pl.ds(0, side - 1)])
 
@@ -450,12 +475,12 @@
         block = gin.at[core, my_big]
         fan_a(lambda to: block, block, GIN_A, tower_a_in.at[pl.ds(0, side - 1)])
 
-    beside = {1: tower_second, 3: tower_x}
+    beside = {0: tower_second, 3: tower_x}
     for c in range(n_chunks):
         token_grads(c)
         if c in beside:
             beside[c]()
-    beside = {1: gather_x, 2: gather_b}
+    beside = {1: gather_b}
     for c in range(n_chunks):
         pooled_grads(c)
         if c > 0:
@@ -463,7 +488,6 @@
         if c in beside:
             beside[c]()
 
-    last = n_chunks - 1
     took(dpooled_t.at[last, 1], rs.at[DPOOL + last])
     for i in range(1, side):
         to = lax.rem(a + i, side)
@@ -472,27 +496,26 @@
     sent.append((ga_in.at[pl.ds(0, side - 1)], GRAD_A))
     ga_in[a] = row_grads(last, a).astype(BF16)
 
+    took(ga_in.at[pl.ds(0, side - 1)], rs.at[GRAD_A])
+    total = sum_of(ga_in, side)
+    for k in range(side):
+        gb_out[k] = total[:, k * span : (k + 1) * span].astype(BF16)
+    fan_b(lambda to: gb_out.at[to], gb_in.at[b], GRAD_B, gb_in.at[pl.ds(0, side - 1)])
+    gb_in[b] = gb_out[b]
     took(tower_a_in.at[pl.ds(0, side - 1)], rs.at[GIN_A])
     to_sibling(gin.at[core], gin.at[core], GIN_S)
     took(gto_e.at[pl.ds(0, n_expert - 1)], rs.at[GTO_E])
     gtout_ref[...] = sum_of(gto_e, n_expert)
+    took(gb_in.at[pl.ds(0, side - 1)], rs.at[GRAD_B])
+    gx_out[...] = sum_of(gb_in, side).T.astype(BF16).reshape(n_x, per, LANES)
+    fan_x(lambda to: gx_out.at[to], gx_in.at[x], GRAD_X, gx_in.at[pl.ds(0, n_x - 1)])
+    gx_in[x] = gx_out[x]
     took(gin.at[0], rs.at[GIN_S])
     gin_outs = [
         pltpu.make_async_copy(gin.at[h], gin_hbm.at[:, pl.ds(h * t_cols, t_cols)], local_sem.at[3 + h]) for h in range(2)
     ]
     for copy in gin_outs:
         copy.start()
-
-    took(ga_in.at[pl.ds(0, side - 1)], rs.at[GRAD_A])
-    total = sum_of(ga_in, side)
-    for k in range(side):
-        gb_out[k] = total[:, k * span : (k + 1) * span].astype(BF16)
-    fan_b(lambda to: gb_out.at[to], gb_in.at[b], GRAD_B, gb_in.at[pl.ds(0, side - 1)])
-    gb_in[b] = gb_out[b]
-    took(gb_in.at[pl.ds(0, side - 1)], rs.at[GRAD_B])
-    gx_out[...] = sum_of(gb_in, side).T.astype(BF16).reshape(n_x, per, LANES)
-    fan_x(lambda to: gx_out.at[to], gx_in.at[x], GRAD_X, gx_in.at[pl.ds(0, n_x - 1)])
-    gx_in[x] = gx_out[x]
     took(gx_in.at[pl.ds(0, n_x - 1)], rs.at[GRAD_X])
     grows_ref[...] = sum_of(gx_in, n_x)
 
@@ -502,10 +525,24 @@
         copy.wait()
 
 
-def finish(gin_ref, grows_ref, gto_ref, gin_out, grows_out, gto_out):
-    gin_out[...] = gin_ref[...].astype(F32)
-    grows_out[...] = grows_ref[...]
-    gto_out[...] = gto_ref[...]
+def finish(gin_hbm, grows_hbm, gto_hbm, gin_out, grows_out, gto_out, narrow, wide, sem_in, sem_out):
+    n = sem_in.shape[0] - 2
+    step = narrow.shape[0] // n
+    pieces = [pl.ds(i * step, step) for i in range(n)]
+    ins = [pltpu.make_async_copy(gin_hbm.at[p], narrow.at[p], sem_in.at[i]) for i, p in enumerate(pieces)]
+    outs = [pltpu.make_async_copy(wide.at[p], gin_out.at[p], sem_out.at[i]) for i, p in enumerate(pieces)]
+    small = [
+        pltpu.make_async_copy(grows_hbm, grows_out, sem_in.at[n]),
+        pltpu.make_async_copy(gto_hbm, gto_out, sem_in.at[n + 1]),
+    ]
+    for copy in ins + small:
+        copy.start()
+    for i, p in enumerate(pieces):
+        ins[i].wait()
+        wide[p] = narrow[p].astype(F32)
+        outs[i].start()
+    for copy in outs + small:
+        copy.wait()
 
 
 def per_device(emb_rows, row_ids, route_ids, route_gates, w_in, w_out, tower_in, tower_out, labels):
@@ -527,7 +564,6 @@
     m_rows = slots // HALVES
     t_rows = eout // n_table
     t_cols = tasks * tw // 2
-    x_cols = t_cols // n_x
     vmem = pl.BlockSpec(memory_space=pltpu.VMEM)
     hbm = pl.BlockSpec(memory_space=pl.ANY)
     dma = pltpu.SemaphoreType.DMA
@@ -541,6 +577,7 @@
         pltpu.VMEM((side, side, span, LANES), BF16),
         pltpu.VMEM((n_chunks, CHUNK, LANES), F32),
         pltpu.VMEM((n_chunks, CHUNK, LANES), F32),
+        pltpu.VMEM((n_chunks, CHUNK, LANES), F32),
         pltpu.VMEM((2, samples, slots), BF16),
         pltpu.VMEM((samples, slots), BF16),
         pltpu.VMEM((slots, samples), BF16),
@@ -548,6 +585,7 @@
         pltpu.VMEM((n_chunks, n_expert, cap, CHUNK), BF16),
         pltpu.VMEM((n_chunks, n_expert, cap, CHUNK), BF16),
         pltpu.VMEM((m_rows, eout), F32),
+        pltpu.VMEM((slots, hid), F32),
         pltpu.VMEM((HALVES, m_rows, hid), BF16),
         pltpu.VMEM((n_expert, cap, eout), BF16),
         pltpu.VMEM((n_expert, cap, eout), BF16),
@@ -559,8 +597,8 @@
         pltpu.VMEM((side, side * t_rows, t_cols), BF16),
         pltpu.VMEM((side, t_rows, t_cols), BF16),
         pltpu.VMEM((side, t_rows, t_cols), BF16),
-        pltpu.VMEM((n_x, t_rows, x_cols), BF16),
-        pltpu.VMEM((n_x, t_rows, x_cols), BF16),
+        pltpu.VMEM((t_rows, t_cols), BF16),
+        pltpu.VMEM((n_x, t_rows, t_cols), BF16),
         pltpu.VMEM((2, eout, t_cols), BF16),
         pltpu.VMEM((3, tasks, tw), F32),
         pltpu.VMEM((side, tasks, tw), F32),
@@ -568,7 +606,6 @@
         pltpu.VMEM((n_expert, tasks, tw), F32),
         pltpu.VMEM((n_expert, cap, eout), BF16),
         pltpu.VMEM((n_expert, cap, eout), BF16),
-        pltpu.VMEM((HALVES, m_rows, hid), BF16),
         pltpu.VMEM((n_chunks, n_expert, cap, CHUNK), BF16),
         pltpu.VMEM((n_chunks, n_expert, cap, CHUNK), BF16),
         pltpu.VMEM((n_chunks, 2, LANES, CHUNK), BF16),
@@ -607,18 +644,21 @@
         w_out[0],
         tower_in,
     )
-    whole = lambda shape: pl.BlockSpec(shape, lambda i: (0, 0))
-    piece = pl.BlockSpec((eout // 4, tasks * tw), lambda i: (i, 0))
     gin, grows, gtout = pl.pallas_call(
         finish,
-        grid=(4,),
         out_shape=(
             jax.ShapeDtypeStruct((eout, tasks * tw), F32),
             jax.ShapeDtypeStruct((per, dim), F32),
             jax.ShapeDtypeStruct((tasks, tw), F32),
         ),
-        in_specs=[piece, whole((per, dim)), whole((tasks, tw))],
-        out_specs=(piece, whole((per, dim)), whole((tasks, tw))),
+        in_specs=[hbm] * 3,
+        out_specs=(hbm,) * 3,
+        scratch_shapes=[
+            pltpu.VMEM((eout, tasks * tw), BF16),
+            pltpu.VMEM((eout, tasks * tw), F32),
+            dma((10,)),
+            dma((8,)),
+        ],
     )(gin, grows, gtout)
     return grows, gin, gtout
 

time: 114 us -> 101 us (0.89)
  Pallas kernels: 113 us -> 100 us
    pallas_call x1, Pallas kernels: 109 us -> 97 us  [per_device(): pl.pallas_call(functools.partial(kernel, n_table, n_expert), out_shape=(j...]
where the time goes in v3:
time: 101 us
  Pallas kernels  100 us (99%)
    pallas_call x1, Pallas kernels, per_device(): pl.pallas_call(functools.partial(kernel, n_table, n_expert), out_shape=(j...  97 us
    pallas_call x1, Pallas kernels, per_device(): pl.pallas_call(finish, out_shape=(jax.ShapeDtypeStruct((eout, tasks * tw)...  3.15 us

profile of v3, /device:TPU:0, one launch (start us, length us, event | category | flops | bytes accessed | tf_op | source)
XLA Modules:
  0.0 100.9 jit_solution(14830531078456377202)
XLA Ops:
  0.6 97.0 %shard_map.112 = (f32[64,128]{1,0:T(8,128)}, bf16[512,2048]{1,0:T(8,128)(2,1)}, f32[8,256]{1,0:T(8,128)}) custom-call(s32[32,128]{1,0:T(8,128)} %bitcast.12, bf16[4,2,64,128]{3,2,1,0:T(8,128)(2,1)} %bitcast.11, s32[2,128]{1,0:T(2,128)} %bitcast.14, f32[2,128]{1,0:T(2,128)} %bitcast.15, f32[8,128]{1,0:T(8,128)} %bitcast.13, f32[8,256]{1,0:T(8,128)} %tout_ref.1, ...), custom_call_target="tpu_custom_call" | custom-call | tf_op jit(solution)/shard_map/pallas_call | solution.py:623
  97.6 3.1 %shard_map.113 = (f32[512,2048]{1,0:T(8,128)}, f32[64,128]{1,0:T(8,128)}, f32[8,256]{1,0:T(8,128)}) custom-call(bf16[512,2048]{1,0:T(8,128)(2,1)} %get-tuple-element.9.gin_hbm, f32[64,128]{1,0:T(8,128)} %get-tuple-element.10.grows_hbm, f32[8,256]{1,0:T(8,128)} %get-tuple-element.11.gto_hbm), custom_call_target="tpu_custom_call" | custom-call | tf_op jit(solution)/shard_map/pallas_call | solution.py:647

commit v4 on v3

--- a/solution.py
+++ b/solution.py
@@ -14,18 +14,21 @@
 LANES = 128
 HALVES = 2
 CHUNK = 256
-TILE = 2048
+WIDE = 512
+TILE = 4096
 
 
 IDS, EMB_A, EMB_B, COMB, DTOW, GTO_A, GTO_B, GTO_E = range(8)
-TOW_A, TOW_B, TOW_X, GIN_B, GIN_A, GIN_S = range(8, 14)
+TOW_A, TOW_B, TOW_X, GIN_B, GIN_X = range(8, 13)
 BACK, GRAD_A, GRAD_B, GRAD_X = range(15, 19)
 DBOX = 20
 PART = 24
 DBACK = 28
 DPOOL = 32
 BOX = 36
-N_SEMS = 40
+GIN_A = 40
+GIN_S = 44
+N_SEMS = 48
 
 
 def dot(a, b):
@@ -36,30 +39,36 @@
     return lax.dot_general(a, b, (((1,), (1,)), ((), ())), preferred_element_type=F32)
 
 
-def silu_grad(pre, sig):
-    return sig * (1.0 + pre * (1.0 - sig))
+def silu_and_slope(pre):
+    sig = 0.5 * jnp.tanh(0.5 * pre) + 0.5
+    out = pre * sig
+    return out, sig + out * (1.0 - sig)
 
 
 def kernel(
     n_table,
     n_expert,
-    ids_ref,
-    emb_ref,
-    route_ref,
-    gate_ref,
-    labels_ref,
-    tout_ref,
+    ids_hbm,
+    emb_hbm,
+    route_hbm,
+    gate_hbm,
+    labels_hbm,
+    tout_hbm,
     w_in_hbm,
     w_out_hbm,
     tin_hbm,
-    grows_ref,
+    grows_hbm,
     gin_hbm,
-    gtout_ref,
+    gtout_hbm,
     w_in,
     w_out,
     tin,
     ids,
+    route,
     narrow,
+    tout,
+    grows,
+    gtout,
     counts,
     rows,
     part_out,
@@ -119,7 +128,7 @@
     b = jnp.where(first, t % side, t // side)
     a_step = jnp.where(first, side, 1)
     b_step = jnp.where(first, 1, side)
-    lookups, batch = ids_ref.shape
+    lookups, batch = ids.shape[1:]
     n_chunks = outbox.shape[0]
     width = n_chunks * CHUNK
     n_feat = width // LANES
@@ -128,8 +137,8 @@
     slots = n_expert * cap
     hid = w_in.shape[1]
     eout = w_out.shape[1]
-    tasks, tw = tout_ref.shape
-    per = emb_ref.shape[2]
+    tasks, tw = tout.shape
+    per = rows.shape[3]
     span = n_x * per
     cols = n_table * span
     rel_per = n_expert // HALVES
@@ -191,10 +200,6 @@
             total += ref[i].astype(F32)
         return total
 
-    w_in_copy = pltpu.make_async_copy(w_in_hbm, w_in, local_sem.at[0])
-    w_out_copy = pltpu.make_async_copy(w_out_hbm, w_out, local_sem.at[1])
-    tin_copy = pltpu.make_async_copy(tin_hbm, tin, local_sem.at[2])
-
     barrier = pltpu.get_barrier_semaphore()
     for i in range(1, side):
         for to_t in (lax.rem(a + i, side) * a_step + b * b_step, a * a_step + lax.rem(b + i, side) * b_step):
@@ -202,8 +207,24 @@
     for i in others:
         pl.semaphore_signal(barrier, inc=1, device_id=(t, rel_expert(i)), device_id_type=MESH)
 
-    ids[0] = ids_ref[...]
-    rows[b, a] = emb_ref[:, core].reshape(span, LANES)
+    def local(src, dst, k):
+        return pltpu.make_async_copy(src, dst, local_sem.at[k])
+
+    ids_copy = local(ids_hbm, ids.at[0], 0)
+    emb_copy = local(emb_hbm.at[:, core], rows.at[b, a], 1)
+    small = [
+        local(route_hbm, route, 2),
+        local(gate_hbm, narrow.at[pl.ds(0, 2)], 3),
+        local(labels_hbm, narrow.at[pl.ds(8, tasks)], 4),
+        local(tout_hbm, tout, 5),
+    ]
+    w_in_copy = local(w_in_hbm, w_in, 6)
+    w_out_copy = local(w_out_hbm, w_out, 7)
+    tin_copy = local(tin_hbm, tin, 8)
+    for copy in [emb_copy, ids_copy] + small:
+        copy.start()
+    emb_copy.wait()
+    ids_copy.wait()
     pl.semaphore_wait(barrier, 2 * (side - 1) + n_expert - 1)
 
     fan_a(lambda to: rows.at[b, a], rows.at[b, a], EMB_A, rows.at[0, pl.ds(0, side - 1)])
@@ -212,15 +233,14 @@
     w_out_copy.start()
     tin_copy.start()
 
-    narrow[...] = jnp.zeros_like(narrow)
-    narrow[0:2] = route_ref[...].astype(F32)
-    narrow[8:10] = gate_ref[...]
-    narrow[16 : 16 + tasks] = labels_ref[...]
+    for copy in small:
+        copy.wait()
     columns = narrow[...].T
+    named_by = jnp.concatenate([route[...].astype(F32), jnp.zeros((LANES - 2, batch), F32)], axis=0).T.astype(jnp.int32)
     lane = lax.broadcasted_iota(jnp.int32, (batch, LANES), 1)
     slot_lane = lax.broadcasted_iota(jnp.int32, (batch, slots), 1)
-    r0, r1 = columns[:, 0:1].astype(jnp.int32), columns[:, 1:2].astype(jnp.int32)
-    gate0, gate1 = columns[:, 8:9], columns[:, 9:10]
+    r0, r1 = named_by[:, 0:1], named_by[:, 1:2]
+    gate0, gate1 = columns[:, 0:1], columns[:, 1:2]
     named0, named1 = lane == r0, lane == r1
     named = jnp.where(named0 | named1, 1.0, 0.0).astype(BF16)
     earlier = jnp.where(
@@ -334,9 +354,9 @@
             at = pl.ds(pl.multiple_of(n * tile, tile), tile)
             pre = dot(inbox[last, mine].reshape(m_rows, CHUNK), w_in[last * CHUNK : (last + 1) * CHUNK, at])
             pre += pre_acc[half * m_rows : (half + 1) * m_rows, at]
-            sig = jax.nn.sigmoid(pre)
-            slope[half, :, at] = silu_grad(pre, sig).astype(BF16)
-            acc[...] += dot((pre * sig).astype(BF16), w_out[at, :])
+            hidden, grad = silu_and_slope(pre)
+            slope[half, :, at] = grad.astype(BF16)
+            acc[...] += dot(hidden.astype(BF16), w_out[at, :])
 
         made[mine] = acc[...].astype(BF16).reshape(rel_per, cap, eout)
         for i in others:
@@ -354,13 +374,12 @@
     per_half = tasks // 2
     for k in range(tasks):
         pre = dot(combined, tin[:, k * tw : (k + 1) * tw])
-        sig = jax.nn.sigmoid(pre)
-        units = pre * sig
-        out_row = tout_ref[k : k + 1, :]
+        units, unit_slope = silu_and_slope(pre)
+        out_row = tout[k : k + 1, :]
         logit = jnp.sum(units * out_row, axis=1, keepdims=True)
-        dlogit = (jax.nn.sigmoid(logit) - columns[:, 16 + k : 17 + k]) / tasks
+        dlogit = (jax.nn.sigmoid(logit) - columns[:, 8 + k : 9 + k]) / tasks
         gto_out[0, k : k + 1, :] = jnp.sum(dlogit * units, axis=0, keepdims=True)
-        grad = (dlogit * out_row * silu_grad(pre, sig)).astype(BF16)
+        grad = (dlogit * out_row * unit_slope).astype(BF16)
         dtow[k // per_half, :, (k % per_half) * tw : (k % per_half + 1) * tw] = grad
     to_sibling(comb.at[0], comb.at[1], COMB)
     to_sibling(dtow.at[sib], dtow_own.at[1], DTOW)
@@ -393,6 +412,15 @@
     fan_a(lambda to: tower_a_out.at[to], tower_a_in.at[a], TOW_A, tower_a_in.at[pl.ds(0, side - 1)])
     tower_a_in[a] = tower_a_out[a]
 
+    n_wide = width // WIDE
+
+    def token_grads(half, c):
+        block = dot_nt(slope[half], w_in[c * WIDE : (c + 1) * WIDE, :])
+        drows[c, half * rel_per : (half + 1) * rel_per] = block.astype(BF16).reshape(rel_per, cap, WIDE)
+        for i in reversed(others):
+            if i // rel_per == half:
+                remote(drows.at[c, i], dback.at[c, e], DBACK + c, DBACK + c, t, rel_expert(i)).start()
+
     def tower_first():
         took(tower_a_in.at[pl.ds(0, side - 1)], rs.at[TOW_A])
         took(gto_a.at[pl.ds(0, side - 1)], rs.at[GTO_A])
@@ -405,8 +433,6 @@
 
     for half in reversed(range(HALVES)):
         took(din.at[arrived(half)], rs.at[DBOX + half])
-        if half == 0:
-            tower_first()
         mine = slice(half * rel_per, (half + 1) * rel_per)
 
         @pl.loop(0, hid // tile)
@@ -415,49 +441,53 @@
             dhid = dot_nt(din[mine].reshape(m_rows, eout), w_out[at, :])
             slope[half, :, at] = (dhid * slope[half, :, at].astype(F32)).astype(BF16)
 
-    def token_grads(c):
-        for half in range(HALVES):
-            block = dot_nt(slope[half], w_in[c * CHUNK : (c + 1) * CHUNK, :])
-            drows[c, half * rel_per : (half + 1) * rel_per] = block.astype(BF16).reshape(rel_per, cap, CHUNK)
-        for i in others:
-            remote(drows.at[c, i], dback.at[c, e], DBACK + c, DBACK + c, t, rel_expert(i)).start()
+        if half == 0:
+            tower_first()
+        for c in range(n_wide):
+            token_grads(half, c)
+
+    for c in range(n_wide):
+        dback[c, e] = drows[c, me]
         sent.append((drows.at[c, pl.ds(0, n_expert - 1)], DBACK + c))
-        dback[c, e] = drows[c, me]
 
     def pooled_grads(c):
         took(dback.at[c, pl.ds(0, n_expert - 1)], rs.at[DBACK + c])
-        got = dot(place_sum[...], dback[c].reshape(slots, CHUNK)).astype(BF16).astype(F32)
-        for f in range(per_chunk):
+        got = dot(place_sum[...], dback[c].reshape(slots, WIDE)).astype(BF16).astype(F32)
+        for f in range(WIDE // LANES):
             dpooled_t[c, 0, :, f * batch : (f + 1) * batch] = got[:, f * LANES : (f + 1) * LANES].T.astype(BF16)
         to_sibling(dpooled_t.at[c, 0], dpooled_t.at[c, 1], DPOOL + c)
 
-    def row_grads(c, at_a):
-        total = None
-        for s in range(2):
-            parts = [
-                counts[s, c * CHUNK : (c + 1) * CHUNK, pl.ds(pl.multiple_of((bb * side + at_a) * span, span), span)]
-                for bb in range(side)
-            ]
-            term = dot(dpooled_t[c, s], jnp.concatenate(parts, axis=1))
-            total = term if total is None else total + term
-        return total if c == 0 else total + grad_acc[at_a]
-
-    def add_chunk(c):
-        took(dpooled_t.at[c, 1], rs.at[DPOOL + c])
+    def row_grads(c, s, at_a):
+        parts = [
+            counts[s, c * WIDE : (c + 1) * WIDE, pl.ds(pl.multiple_of((bb * side + at_a) * span, span), span)]
+            for bb in range(side)
+        ]
+        return dot(dpooled_t[c, s], jnp.concatenate(parts, axis=1))
+
+    def add_chunk(c, s):
+        if s == 1:
+            took(dpooled_t.at[c, 1], rs.at[DPOOL + c])
         for at_a in range(side):
-            grad_acc[at_a] = row_grads(c, at_a)
+            part = row_grads(c, s, at_a)
+            grad_acc[at_a] = part if c == 0 and s == 0 else grad_acc[at_a] + part
 
     def gin_rows(at, n):
         return pl.ds(pl.multiple_of(at * t_rows, t_rows), n * t_rows)
 
+    x_cols = t_cols // n_x
+    x_at = pl.ds(pl.multiple_of(x * x_cols, x_cols), x_cols)
     my_rows, my_big = gin_rows(a * side + b, 1), gin_rows(a * side, side)
+    from_b = gin.at[0, pl.ds(0, (side - 1) * t_rows), pl.ds(0, x_cols)]
+    from_x = gin.at[0, pl.ds(0, side * t_rows), pl.ds(0, (n_x - 1) * x_cols)]
 
     def tower_second():
         took(tower_b_in.at[pl.ds(0, side - 1)], rs.at[TOW_B])
         took(gto_b.at[pl.ds(0, side - 1)], rs.at[GTO_B])
-        tower_x_out[...] = sum_of(tower_b_in, side).astype(BF16)
-        fan_x(lambda to: tower_x_out, tower_x_in.at[x], TOW_X, tower_x_in.at[pl.ds(0, n_x - 1)])
-        tower_x_in[x] = tower_x_out[...]
+        total = sum_of(tower_b_in, side)
+        for k in range(n_x):
+            tower_x_out[k] = total[:, k * x_cols : (k + 1) * x_cols].astype(BF16)
+        fan_x(lambda to: tower_x_out.at[to], tower_x_in.at[x], TOW_X, tower_x_in.at[pl.ds(0, n_x - 1)])
+        tower_x_in[x] = tower_x_out[x]
         gto_out[2] = sum_of(gto_b, side)
         for i in others:
             remote(gto_out.at[2], gto_e.at[e], GTO_E, GTO_E, t, rel_expert(i)).start()
@@ -466,62 +496,90 @@
 
     def tower_x():
         took(tower_x_in.at[pl.ds(0, n_x - 1)], rs.at[TOW_X])
-        gin[core, my_rows] = sum_of(tower_x_in, n_x).astype(BF16)
-        block = gin.at[core, my_rows]
-        fan_b(lambda to: block, block, GIN_B, tower_b_in.at[pl.ds(0, side - 1)])
+        gin[core, my_rows, x_at] = sum_of(tower_x_in, n_x).astype(BF16)
+        block = gin.at[core, my_rows, x_at]
+        fan_b(lambda to: block, block, GIN_B, from_b)
 
     def gather_b():
-        took(tower_b_in.at[pl.ds(0, side - 1)], rs.at[GIN_B])
+        took(from_b, rs.at[GIN_B])
+        block = gin.at[core, my_big, x_at]
+        fan_x(lambda to: block, block, GIN_X, from_x)
+
+    gin_outs = []
+
+    def gin_out(half, at_a):
+        at = gin_rows(at_a * side, side)
+        copy = local(gin.at[half, at], gin_hbm.at[at, pl.ds(pl.multiple_of(half * t_cols, t_cols), t_cols)], 9 + len(gin_outs))
+        copy.start()
+        gin_outs.append(copy)
+
+    def whole(i):
+        at_a = lax.rem(a + i, side)
+        block = gin.at[core, gin_rows(at_a * side, side)]
+        to_sibling(block, block, GIN_S + i)
+        gin_out(core, at_a)
+
+    def gather_x():
+        took(from_x, rs.at[GIN_X])
         block = gin.at[core, my_big]
-        fan_a(lambda to: block, block, GIN_A, tower_a_in.at[pl.ds(0, side - 1)])
-
-    beside = {0: tower_second, 3: tower_x}
-    for c in range(n_chunks):
-        token_grads(c)
-        if c in beside:
-            beside[c]()
-    beside = {1: gather_b}
-    for c in range(n_chunks):
+        for i in range(1, side):
+            to = lax.rem(a + i, side)
+            remote(block, block, GIN_A + i, GIN_A + side - i, to * a_step + b * b_step, e).start()
+            sent.append((block, GIN_A + i))
+        whole(0)
+
+    def gather_a(i):
+        took(gin.at[0, my_big], rs.at[GIN_A + i])
+        whole(i)
+
+    def from_sibling(i):
+        took(gin.at[0, my_big], rs.at[GIN_S + i])
+        gin_out(sib, lax.rem(b + i, side))
+
+    tower_second()
+    last = n_wide - 1
+    for c in range(n_wide):
         pooled_grads(c)
         if c > 0:
-            add_chunk(c - 1)
-        if c in beside:
-            beside[c]()
-
+            add_chunk(c - 1, 1)
+        add_chunk(c, 0)
     took(dpooled_t.at[last, 1], rs.at[DPOOL + last])
+    tower_x()
     for i in range(1, side):
         to = lax.rem(a + i, side)
-        ga_out[to] = row_grads(last, to).astype(BF16)
+        ga_out[to] = (grad_acc[to] + row_grads(last, 1, to)).astype(BF16)
         remote(ga_out.at[to], ga_in.at[a], GRAD_A, GRAD_A, to * a_step + b * b_step, e).start()
     sent.append((ga_in.at[pl.ds(0, side - 1)], GRAD_A))
-    ga_in[a] = row_grads(last, a).astype(BF16)
-
+    ga_in[a] = (grad_acc[a] + row_grads(last, 1, a)).astype(BF16)
+
+    gather_b()
+    gather_x()
     took(ga_in.at[pl.ds(0, side - 1)], rs.at[GRAD_A])
     total = sum_of(ga_in, side)
     for k in range(side):
         gb_out[k] = total[:, k * span : (k + 1) * span].astype(BF16)
     fan_b(lambda to: gb_out.at[to], gb_in.at[b], GRAD_B, gb_in.at[pl.ds(0, side - 1)])
     gb_in[b] = gb_out[b]
-    took(tower_a_in.at[pl.ds(0, side - 1)], rs.at[GIN_A])
-    to_sibling(gin.at[core], gin.at[core], GIN_S)
     took(gto_e.at[pl.ds(0, n_expert - 1)], rs.at[GTO_E])
-    gtout_ref[...] = sum_of(gto_e, n_expert)
+    gtout[...] = sum_of(gto_e, n_expert)
+    gto_copy = local(gtout, gtout_hbm, 9 + 2 * side)
+    gto_copy.start()
     took(gb_in.at[pl.ds(0, side - 1)], rs.at[GRAD_B])
     gx_out[...] = sum_of(gb_in, side).T.astype(BF16).reshape(n_x, per, LANES)
     fan_x(lambda to: gx_out.at[to], gx_in.at[x], GRAD_X, gx_in.at[pl.ds(0, n_x - 1)])
     gx_in[x] = gx_out[x]
-    took(gin.at[0], rs.at[GIN_S])
-    gin_outs = [
-        pltpu.make_async_copy(gin.at[h], gin_hbm.at[:, pl.ds(h * t_cols, t_cols)], local_sem.at[3 + h]) for h in range(2)
-    ]
-    for copy in gin_outs:
-        copy.start()
+    for i in range(1, side):
+        gather_a(i)
     took(gx_in.at[pl.ds(0, n_x - 1)], rs.at[GRAD_X])
-    grows_ref[...] = sum_of(gx_in, n_x)
+    grows[...] = sum_of(gx_in, n_x)
+    grows_copy = local(grows, grows_hbm, 10 + 2 * side)
+    grows_copy.start()
+    for i in range(side):
+        from_sibling(i)
 
     for ref, k in sent:
         took(ref, ss.at[k])
-    for copy in gin_outs:
+    for copy in gin_outs + [gto_copy, grows_copy]:
         copy.wait()
 
 
@@ -564,7 +622,8 @@
     m_rows = slots // HALVES
     t_rows = eout // n_table
     t_cols = tasks * tw // 2
-    vmem = pl.BlockSpec(memory_space=pltpu.VMEM)
+    x_cols = t_cols // n_x
+    n_wide = width // WIDE
     hbm = pl.BlockSpec(memory_space=pl.ANY)
     dma = pltpu.SemaphoreType.DMA
     scratch = [
@@ -572,9 +631,13 @@
         pltpu.VMEM((hid, eout), BF16),
         pltpu.VMEM((eout, tasks * tw), BF16),
         pltpu.VMEM((2, tables * bag, samples), jnp.int32),
+        pltpu.VMEM((2, samples), jnp.int32),
         pltpu.VMEM((LANES, samples), F32),
+        pltpu.VMEM((tasks, tw), F32),
+        pltpu.VMEM((per, dim), F32),
+        pltpu.VMEM((tasks, tw), F32),
         pltpu.VMEM((2, width, cols), BF16),
-        pltpu.VMEM((side, side, span, LANES), BF16),
+        pltpu.VMEM((side, side, n_x, per, LANES), BF16),
         pltpu.VMEM((n_chunks, CHUNK, LANES), F32),
         pltpu.VMEM((n_chunks, CHUNK, LANES), F32),
         pltpu.VMEM((n_chunks, CHUNK, LANES), F32),
@@ -597,8 +660,8 @@
         pltpu.VMEM((side, side * t_rows, t_cols), BF16),
         pltpu.VMEM((side, t_rows, t_cols), BF16),
         pltpu.VMEM((side, t_rows, t_cols), BF16),
-        pltpu.VMEM((t_rows, t_cols), BF16),
-        pltpu.VMEM((n_x, t_rows, t_cols), BF16),
+        pltpu.VMEM((n_x, t_rows, x_cols), BF16),
+        pltpu.VMEM((n_x, t_rows, x_cols), BF16),
         pltpu.VMEM((2, eout, t_cols), BF16),
         pltpu.VMEM((3, tasks, tw), F32),
         pltpu.VMEM((side, tasks, tw), F32),
@@ -606,9 +669,9 @@
         pltpu.VMEM((n_expert, tasks, tw), F32),
         pltpu.VMEM((n_expert, cap, eout), BF16),
         pltpu.VMEM((n_expert, cap, eout), BF16),
-        pltpu.VMEM((n_chunks, n_expert, cap, CHUNK), BF16),
-        pltpu.VMEM((n_chunks, n_expert, cap, CHUNK), BF16),
-        pltpu.VMEM((n_chunks, 2, LANES, CHUNK), BF16),
+        pltpu.VMEM((n_wide, n_expert, cap, WIDE), BF16),
+        pltpu.VMEM((n_wide, n_expert, cap, WIDE), BF16),
+        pltpu.VMEM((n_wide, 2, LANES, WIDE), BF16),
         pltpu.VMEM((side, LANES, side * span), F32),
         pltpu.VMEM((side, LANES, side * span), BF16),
         pltpu.VMEM((side, LANES, side * span), BF16),
@@ -616,7 +679,7 @@
         pltpu.VMEM((side, LANES, span), BF16),
         pltpu.VMEM((n_x, per, LANES), BF16),
         pltpu.VMEM((n_x, per, LANES), BF16),
-        dma((5,)),
+        dma((11 + 2 * side,)),
         dma((N_SEMS,)),
         dma((N_SEMS,)),
     ]
@@ -627,8 +690,8 @@
             jax.ShapeDtypeStruct((eout, tasks * tw), BF16),
             jax.ShapeDtypeStruct((tasks, tw), F32),
         ),
-        in_specs=[vmem] * 6 + [hbm] * 3,
-        out_specs=(vmem, hbm, vmem),
+        in_specs=[hbm] * 9,
+        out_specs=(hbm,) * 3,
         scratch_shapes=scratch,
         compiler_params=pltpu.CompilerParams(
             collective_id=0, has_side_effects=True, vmem_limit_bytes=VMEM_LIMIT

time: 101 us -> 95.3 us (0.944)
  Pallas kernels: 100 us -> 94.2 us
    pallas_call x1, Pallas kernels: 97 us -> 91 us  [per_device(): pl.pallas_call(functools.partial(kernel, n_table, n_expert), out_shape=(j...]
where the time goes in v4:
time: 95.3 us; the launch traced here: 95 us
  Pallas kernels  94.2 us (99%)
    pallas_call x1, Pallas kernels, per_device(): pl.pallas_call(functools.partial(kernel, n_table, n_expert), out_shape=(j...  91 us
    pallas_call x1, Pallas kernels, per_device(): pl.pallas_call(finish, out_shape=(jax.ShapeDtypeStruct((eout, tasks * tw)...  3.15 us

profile of v4, /device:TPU:0, one launch (start us, length us, event | category | flops | bytes accessed | tf_op | source)
XLA Modules:
  0.0 95.0 jit_solution(3398983128025956916)
XLA Ops:
  0.6 91.0 %shard_map.112 = (f32[64,128]{1,0:T(8,128)}, bf16[512,2048]{1,0:T(8,128)(2,1)}, f32[8,256]{1,0:T(8,128)}) custom-call(s32[32,128]{1,0:T(8,128)} %bitcast.12, bf16[4,2,64,128]{3,2,1,0:T(8,128)(2,1)} %bitcast.11, s32[2,128]{1,0:T(2,128)} %bitcast.14, f32[2,128]{1,0:T(2,128)} %bitcast.15, f32[8,128]{1,0:T(8,128)} %bitcast.13, f32[8,256]{1,0:T(8,128)} %tout_hbm.1, ...), custom_call_target="tpu_custom_call" | custom-call | tf_op jit(solution)/shard_map/pallas_call | solution.py:686
  91.7 3.1 %shard_map.113 = (f32[512,2048]{1,0:T(8,128)}, f32[64,128]{1,0:T(8,128)}, f32[8,256]{1,0:T(8,128)}) custom-call(bf16[512,2048]{1,0:T(8,128)(2,1)} %get-tuple-element.9.gin_hbm, f32[64,128]{1,0:T(8,128)} %get-tuple-element.10.grows_hbm, f32[8,256]{1,0:T(8,128)} %get-tuple-element.11.gto_hbm), custom_call_target="tpu_custom_call" | custom-call | tf_op jit(solution)/shard_map/pallas_call | solution.py:710

commit v5 on v4

--- a/solution.py
+++ b/solution.py
@@ -21,6 +21,7 @@
 IDS, EMB_A, EMB_B, COMB, DTOW, GTO_A, GTO_B, GTO_E = range(8)
 TOW_A, TOW_B, TOW_X, GIN_B, GIN_X = range(8, 13)
 BACK, GRAD_A, GRAD_B, GRAD_X = range(15, 19)
+EMB_B0 = 19
 DBOX = 20
 PART = 24
 DBACK = 28
@@ -228,6 +229,7 @@
     pl.semaphore_wait(barrier, 2 * (side - 1) + n_expert - 1)
 
     fan_a(lambda to: rows.at[b, a], rows.at[b, a], EMB_A, rows.at[0, pl.ds(0, side - 1)])
+    fan_b(lambda to: rows.at[b, a], rows.at[b, a], EMB_B0, rows.at[0, pl.ds(0, side - 1)])
     to_sibling(ids.at[0], ids.at[1], IDS)
     w_in_copy.start()
     w_out_copy.start()
@@ -283,11 +285,14 @@
                 count = jnp.bitwise_and(words[h // 8] >> (4 * (h % 8)), 15)
                 counts[s, f * batch : (f + 1) * batch, h * LANES : (h + 1) * LANES] = count.astype(F32).astype(BF16)
 
-    code = code_of(0)
-    build_counts(0, code, range(n_feat // 2))
+    build_counts(0, code_of(0), range(n_feat))
     took(rows.at[0, pl.ds(0, side - 1)], rs.at[EMB_A])
-    fan_b(lambda to: rows.at[b], rows.at[b], EMB_B, rows.at[pl.ds(0, side - 1)])
-    build_counts(0, code, range(n_feat // 2, n_feat))
+    for i in range(1, side):
+        block = rows.at[b, lax.rem(a + i, side)]
+        for j in range(1, side):
+            to = lax.rem(b + j, side)
+            remote(block, block, EMB_B, EMB_B, a * a_step + to * b_step, e).start()
+    sent.append((rows.at[pl.ds(0, side - 1), pl.ds(0, side - 1)], EMB_B))
     took(ids.at[1], rs.at[IDS])
     build_counts(1, code_of(1), range(n_feat))
 
@@ -300,7 +305,8 @@
     for c in range(n_chunks):
         part_out[c] = partial(1, c, b)
         part_own[c] = partial(0, c, b)
-    took(rows.at[pl.ds(0, side - 1)], rs.at[EMB_B])
+    took(rows.at[0, pl.ds(0, side - 1)], rs.at[EMB_B0])
+    took(rows.at[pl.ds(0, side - 1), pl.ds(0, side - 1)], rs.at[EMB_B])
 
     def all_parts(s, c, total):
         for i in range(1, side):
@@ -386,7 +392,7 @@
     dcomb = sum(dot_nt(dtow[h], tin[:, h * per_half * tw : (h + 1) * per_half * tw]) for h in range(2))
     dent = jnp.concatenate([(gate0 * dcomb).astype(BF16), (gate1 * dcomb).astype(BF16)], axis=0)
     dout[...] = dot(place_both_t[...], dent).astype(BF16).reshape(n_expert, cap, eout)
-    for i in reversed(others):
+    for i in others:
         at = rel_back(i)
         to = rel_expert(i)
         remote(dout.at[to], din.at[at], DBOX, DBOX + at // rel_per, t, to).start()
@@ -417,7 +423,7 @@
     def token_grads(half, c):
         block = dot_nt(slope[half], w_in[c * WIDE : (c + 1) * WIDE, :])
         drows[c, half * rel_per : (half + 1) * rel_per] = block.astype(BF16).reshape(rel_per, cap, WIDE)
-        for i in reversed(others):
+        for i in others:
             if i // rel_per == half:
                 remote(drows.at[c, i], dback.at[c, e], DBACK + c, DBACK + c, t, rel_expert(i)).start()
 
@@ -431,7 +437,7 @@
         fan_b(lambda to: gto_out.at[1], gto_b.at[b], GTO_B, gto_b.at[pl.ds(0, side - 1)])
         gto_b[b] = gto_out[1]
 
-    for half in reversed(range(HALVES)):
+    for half in range(HALVES):
         took(din.at[arrived(half)], rs.at[DBOX + half])
         mine = slice(half * rel_per, (half + 1) * rel_per)
 
@@ -441,7 +447,7 @@
             dhid = dot_nt(din[mine].reshape(m_rows, eout), w_out[at, :])
             slope[half, :, at] = (dhid * slope[half, :, at].astype(F32)).astype(BF16)
 
-        if half == 0:
+        if half == HALVES - 1:
             tower_first()
         for c in range(n_wide):
             token_grads(half, c)
@@ -542,9 +548,9 @@
         pooled_grads(c)
         if c > 0:
             add_chunk(c - 1, 1)
+            tower_x()
         add_chunk(c, 0)
     took(dpooled_t.at[last, 1], rs.at[DPOOL + last])
-    tower_x()
     for i in range(1, side):
         to = lax.rem(a + i, side)
         ga_out[to] = (grad_acc[to] + row_grads(last, 1, to)).astype(BF16)

time: 95.3 us -> 91.9 us (0.964); the launches traced: 95 us -> 90.5 us
  Pallas kernels: 94.2 us -> 89.7 us
    pallas_call x1, Pallas kernels: 91 us -> 86.5 us  [per_device(): pl.pallas_call(functools.partial(kernel, n_table, n_expert), out_shape=(j...]
where the time goes in v5:
time: 91.9 us; the launch traced here: 90.5 us
  Pallas kernels  89.7 us (98%)
    pallas_call x1, Pallas kernels, per_device(): pl.pallas_call(functools.partial(kernel, n_table, n_expert), out_shape=(j...  86.5 us
    pallas_call x1, Pallas kernels, per_device(): pl.pallas_call(finish, out_shape=(jax.ShapeDtypeStruct((eout, tasks * tw)...  3.15 us

profile of v5, /device:TPU:0, one launch (start us, length us, event | category | flops | bytes accessed | tf_op | source)
XLA Modules:
  0.0 90.5 jit_solution(10319295393123240240)
XLA Ops:
  0.6 86.5 %shard_map.112 = (f32[64,128]{1,0:T(8,128)}, bf16[512,2048]{1,0:T(8,128)(2,1)}, f32[8,256]{1,0:T(8,128)}) custom-call(s32[32,128]{1,0:T(8,128)} %bitcast.12, bf16[4,2,64,128]{3,2,1,0:T(8,128)(2,1)} %bitcast.11, s32[2,128]{1,0:T(2,128)} %bitcast.14, f32[2,128]{1,0:T(2,128)} %bitcast.15, f32[8,128]{1,0:T(8,128)} %bitcast.13, f32[8,256]{1,0:T(8,128)} %tout_hbm.1, ...), custom_call_target="tpu_custom_call" | custom-call | tf_op jit(solution)/shard_map/pallas_call | solution.py:692
  87.2 3.1 %shard_map.113 = (f32[512,2048]{1,0:T(8,128)}, f32[64,128]{1,0:T(8,128)}, f32[8,256]{1,0:T(8,128)}) custom-call(bf16[512,2048]{1,0:T(8,128)(2,1)} %get-tuple-element.9.gin_hbm, f32[64,128]{1,0:T(8,128)} %get-tuple-element.10.grows_hbm, f32[8,256]{1,0:T(8,128)} %get-tuple-element.11.gto_hbm), custom_call_target="tpu_custom_call" | custom-call | tf_op jit(solution)/shard_map/pallas_call | solution.py:716

commit v6 on v5

--- a/solution.py
+++ b/solution.py
@@ -29,7 +29,8 @@
 BOX = 36
 GIN_A = 40
 GIN_S = 44
-N_SEMS = 48
+GIN_A2, GIN_X2, GIN_S2 = 48, 49, 50
+N_SEMS = 51
 
 
 def dot(a, b):
@@ -285,7 +286,9 @@
                 count = jnp.bitwise_and(words[h // 8] >> (4 * (h % 8)), 15)
                 counts[s, f * batch : (f + 1) * batch, h * LANES : (h + 1) * LANES] = count.astype(F32).astype(BF16)
 
-    build_counts(0, code_of(0), range(n_feat))
+    code = code_of(0)
+    early = 3 * n_feat // 4
+    build_counts(0, code, range(early))
     took(rows.at[0, pl.ds(0, side - 1)], rs.at[EMB_A])
     for i in range(1, side):
         block = rows.at[b, lax.rem(a + i, side)]
@@ -293,6 +296,7 @@
             to = lax.rem(b + j, side)
             remote(block, block, EMB_B, EMB_B, a * a_step + to * b_step, e).start()
     sent.append((rows.at[pl.ds(0, side - 1), pl.ds(0, side - 1)], EMB_B))
+    build_counts(0, code, range(early, n_feat))
     took(ids.at[1], rs.at[IDS])
     build_counts(1, code_of(1), range(n_feat))
 
@@ -375,7 +379,8 @@
     took(returned.at[pl.ds(0, n_expert - 1)], rs.at[BACK])
 
     answers = returned[...].reshape(slots, eout)
-    combined = (gate0 * dot(place[0], answers) + gate1 * dot(place[1], answers)).astype(BF16)
+    both = dot(place[...].reshape(2 * batch, slots), answers)
+    combined = (gate0 * both[:batch] + gate1 * both[batch:]).astype(BF16)
     comb[0] = combined
     per_half = tasks // 2
     for k in range(tasks):
@@ -439,6 +444,8 @@
 
     for half in range(HALVES):
         took(din.at[arrived(half)], rs.at[DBOX + half])
+        if half == HALVES - 1:
+            tower_first()
         mine = slice(half * rel_per, (half + 1) * rel_per)
 
         @pl.loop(0, hid // tile)
@@ -447,8 +454,6 @@
             dhid = dot_nt(din[mine].reshape(m_rows, eout), w_out[at, :])
             slope[half, :, at] = (dhid * slope[half, :, at].astype(F32)).astype(BF16)
 
-        if half == HALVES - 1:
-            tower_first()
         for c in range(n_wide):
             token_grads(half, c)
 
@@ -480,18 +485,23 @@
     def gin_rows(at, n):
         return pl.ds(pl.multiple_of(at * t_rows, t_rows), n * t_rows)
 
-    x_cols = t_cols // n_x
+    x_cols = t_cols // n_x // 2
+    g_cols = t_cols // 2
     x_at = pl.ds(pl.multiple_of(x * x_cols, x_cols), x_cols)
     my_rows, my_big = gin_rows(a * side + b, 1), gin_rows(a * side, side)
-    from_b = gin.at[0, pl.ds(0, (side - 1) * t_rows), pl.ds(0, x_cols)]
-    from_x = gin.at[0, pl.ds(0, side * t_rows), pl.ds(0, (n_x - 1) * x_cols)]
+    from_b = gin.at[0, :, pl.ds(0, (side - 1) * t_rows), pl.ds(0, x_cols)]
+    from_x = gin.at[0, 0, pl.ds(0, side * t_rows), pl.ds(0, (n_x - 1) * x_cols)]
+    from_a = gin.at[0, 0, pl.ds(0, (side - 1) * side * t_rows), pl.ds(0, x_cols)]
+    from_far_x = gin.at[0, 0, :, pl.ds(0, (n_x - 1) * x_cols)]
 
     def tower_second():
         took(tower_b_in.at[pl.ds(0, side - 1)], rs.at[TOW_B])
         took(gto_b.at[pl.ds(0, side - 1)], rs.at[GTO_B])
         total = sum_of(tower_b_in, side)
         for k in range(n_x):
-            tower_x_out[k] = total[:, k * x_cols : (k + 1) * x_cols].astype(BF16)
+            for h in range(2):
+                at = h * g_cols + k * x_cols
+                tower_x_out[k, h] = total[:, at : at + x_cols].astype(BF16)
         fan_x(lambda to: tower_x_out.at[to], tower_x_in.at[x], TOW_X, tower_x_in.at[pl.ds(0, n_x - 1)])
         tower_x_in[x] = tower_x_out[x]
         gto_out[2] = sum_of(gto_b, side)
@@ -502,45 +512,62 @@
 
     def tower_x():
         took(tower_x_in.at[pl.ds(0, n_x - 1)], rs.at[TOW_X])
-        gin[core, my_rows, x_at] = sum_of(tower_x_in, n_x).astype(BF16)
-        block = gin.at[core, my_rows, x_at]
+        gin[core, :, my_rows, x_at] = sum_of(tower_x_in, n_x).astype(BF16)
+        block = gin.at[core, :, my_rows, x_at]
         fan_b(lambda to: block, block, GIN_B, from_b)
 
     def gather_b():
         took(from_b, rs.at[GIN_B])
-        block = gin.at[core, my_big, x_at]
+        near = gin.at[core, 1, my_big, x_at]
+        fan_a(lambda to: near, near, GIN_A2, from_a)
+        block = gin.at[core, 0, my_big, x_at]
         fan_x(lambda to: block, block, GIN_X, from_x)
 
     gin_outs = []
 
-    def gin_out(half, at_a):
-        at = gin_rows(at_a * side, side)
-        copy = local(gin.at[half, at], gin_hbm.at[at, pl.ds(pl.multiple_of(half * t_cols, t_cols), t_cols)], 9 + len(gin_outs))
+    def gin_out(half, h, at):
+        to = pl.ds(pl.multiple_of(half * t_cols + h * g_cols, g_cols), g_cols)
+        copy = local(gin.at[half, h, at], gin_hbm.at[at, to], 9 + len(gin_outs))
         copy.start()
         gin_outs.append(copy)
 
     def whole(i):
-        at_a = lax.rem(a + i, side)
-        block = gin.at[core, gin_rows(at_a * side, side)]
+        at = gin_rows(lax.rem(a + i, side) * side, side)
+        block = gin.at[core, 0, at]
         to_sibling(block, block, GIN_S + i)
-        gin_out(core, at_a)
+        gin_out(core, 0, at)
 
     def gather_x():
         took(from_x, rs.at[GIN_X])
-        block = gin.at[core, my_big]
+        block = gin.at[core, 0, my_big]
         for i in range(1, side):
             to = lax.rem(a + i, side)
             remote(block, block, GIN_A + i, GIN_A + side - i, to * a_step + b * b_step, e).start()
             sent.append((block, GIN_A + i))
         whole(0)
 
+    def gather_far():
+        took(from_a, rs.at[GIN_A2])
+        block = gin.at[core, 1, :, x_at]
+        fan_x(lambda to: block, block, GIN_X2, from_far_x)
+
     def gather_a(i):
-        took(gin.at[0, my_big], rs.at[GIN_A + i])
+        took(gin.at[0, 0, my_big], rs.at[GIN_A + i])
         whole(i)
 
+    def gather_far_x():
+        took(from_far_x, rs.at[GIN_X2])
+        block = gin.at[core, 1]
+        to_sibling(block, block, GIN_S2)
+        gin_out(core, 1, pl.ds(0, eout))
+
     def from_sibling(i):
-        took(gin.at[0, my_big], rs.at[GIN_S + i])
-        gin_out(sib, lax.rem(b + i, side))
+        took(gin.at[0, 0, my_big], rs.at[GIN_S + i])
+        gin_out(sib, 0, gin_rows(lax.rem(b + i, side) * side, side))
+
+    def far_from_sibling():
+        took(gin.at[0, 1], rs.at[GIN_S2])
+        gin_out(sib, 1, pl.ds(0, eout))
 
     tower_second()
     last = n_wide - 1
@@ -549,14 +576,15 @@
         if c > 0:
             add_chunk(c - 1, 1)
             tower_x()
-        add_chunk(c, 0)
+        if c < last:
+            add_chunk(c, 0)
     took(dpooled_t.at[last, 1], rs.at[DPOOL + last])
     for i in range(1, side):
         to = lax.rem(a + i, side)
-        ga_out[to] = (grad_acc[to] + row_grads(last, 1, to)).astype(BF16)
+        ga_out[to] = (grad_acc[to] + row_grads(last, 0, to) + row_grads(last, 1, to)).astype(BF16)
         remote(ga_out.at[to], ga_in.at[a], GRAD_A, GRAD_A, to * a_step + b * b_step, e).start()
     sent.append((ga_in.at[pl.ds(0, side - 1)], GRAD_A))
-    ga_in[a] = (grad_acc[a] + row_grads(last, 1, a)).astype(BF16)
+    ga_in[a] = (grad_acc[a] + row_grads(last, 0, a) + row_grads(last, 1, a)).astype(BF16)
 
     gather_b()
     gather_x()
@@ -566,9 +594,10 @@
         gb_out[k] = total[:, k * span : (k + 1) * span].astype(BF16)
     fan_b(lambda to: gb_out.at[to], gb_in.at[b], GRAD_B, gb_in.at[pl.ds(0, side - 1)])
     gb_in[b] = gb_out[b]
+    gather_far()
     took(gto_e.at[pl.ds(0, n_expert - 1)], rs.at[GTO_E])
     gtout[...] = sum_of(gto_e, n_expert)
-    gto_copy = local(gtout, gtout_hbm, 9 + 2 * side)
+    gto_copy = local(gtout, gtout_hbm, 11 + 2 * side)
     gto_copy.start()
     took(gb_in.at[pl.ds(0, side - 1)], rs.at[GRAD_B])
     gx_out[...] = sum_of(gb_in, side).T.astype(BF16).reshape(n_x, per, LANES)
@@ -576,12 +605,14 @@
     gx_in[x] = gx_out[x]
     for i in range(1, side):
         gather_a(i)
+    gather_far_x()
     took(gx_in.at[pl.ds(0, n_x - 1)], rs.at[GRAD_X])
     grows[...] = sum_of(gx_in, n_x)
-    grows_copy = local(grows, grows_hbm, 10 + 2 * side)
+    grows_copy = local(grows, grows_hbm, 12 + 2 * side)
     grows_copy.start()
     for i in range(side):
         from_sibling(i)
+    far_from_sibling()
 
     for ref, k in sent:
         took(ref, ss.at[k])
@@ -628,7 +659,7 @@
     m_rows = slots // HALVES
     t_rows = eout // n_table
     t_cols = tasks * tw // 2
-    x_cols = t_cols // n_x
+    x_cols = t_cols // n_x // 2
     n_wide = width // WIDE
     hbm = pl.BlockSpec(memory_space=pl.ANY)
     dma = pltpu.SemaphoreType.DMA
@@ -666,9 +697,9 @@
         pltpu.VMEM((side, side * t_rows, t_cols), BF16),
         pltpu.VMEM((side, t_rows, t_cols), BF16),
         pltpu.VMEM((side, t_rows, t_cols), BF16),
-        pltpu.VMEM((n_x, t_rows, x_cols), BF16),
-        pltpu.VMEM((n_x, t_rows, x_cols), BF16),
-        pltpu.VMEM((2, eout, t_cols), BF16),
+        pltpu.VMEM((n_x, 2, t_rows, x_cols), BF16),
+        pltpu.VMEM((n_x, 2, t_rows, x_cols), BF16),
+        pltpu.VMEM((2, 2, eout, t_cols // 2), BF16),
         pltpu.VMEM((3, tasks, tw), F32),
         pltpu.VMEM((side, tasks, tw), F32),
         pltpu.VMEM((side, tasks, tw), F32),
@@ -685,7 +716,7 @@
         pltpu.VMEM((side, LANES, span), BF16),
         pltpu.VMEM((n_x, per, LANES), BF16),
         pltpu.VMEM((n_x, per, LANES), BF16),
-        dma((11 + 2 * side,)),
+        dma((13 + 2 * side,)),
         dma((N_SEMS,)),
         dma((N_SEMS,)),
     ]

time: 91.9 us -> 92.1 us (level)
  the two profiles are of different devices: /device:TPU:0 before, /device:TPU:1 now
where the time goes in v6:
time: 92.1 us; the launch traced here: 91.9 us
  Pallas kernels  91.1 us (99%)
    pallas_call x1, Pallas kernels, per_device(): pl.pallas_call(functools.partial(kernel, n_table, n_expert), out_shape=(j...  87.9 us
    pallas_call x1, Pallas kernels, per_device(): pl.pallas_call(finish, out_shape=(jax.ShapeDtypeStruct((eout, tasks * tw)...  3.15 us

profile of v6, /device:TPU:1, one launch (start us, length us, event | category | flops | bytes accessed | tf_op | source)
XLA Modules:
  0.0 91.9 jit_solution(8355144358963503310)
XLA Ops:
  0.6 87.9 %shard_map.112 = (f32[64,128]{1,0:T(8,128)}, bf16[512,2048]{1,0:T(8,128)(2,1)}, f32[8,256]{1,0:T(8,128)}) custom-call(s32[32,128]{1,0:T(8,128)} %bitcast.12, bf16[4,2,64,128]{3,2,1,0:T(8,128)(2,1)} %bitcast.11, s32[2,128]{1,0:T(2,128)} %bitcast.14, f32[2,128]{1,0:T(2,128)} %bitcast.15, f32[8,128]{1,0:T(8,128)} %bitcast.13, f32[8,256]{1,0:T(8,128)} %tout_hbm.1, ...), custom_call_target="tpu_custom_call" | custom-call | tf_op jit(solution)/shard_map/pallas_call | solution.py:723
  88.6 3.1 %shard_map.113 = (f32[512,2048]{1,0:T(8,128)}, f32[64,128]{1,0:T(8,128)}, f32[8,256]{1,0:T(8,128)}) custom-call(bf16[512,2048]{1,0:T(8,128)(2,1)} %get-tuple-element.9.gin_hbm, f32[64,128]{1,0:T(8,128)} %get-tuple-element.10.grows_hbm, f32[8,256]{1,0:T(8,128)} %get-tuple-element.11.gto_hbm), custom_call_target="tpu_custom_call" | custom-call | tf_op jit(solution)/shard_map/pallas_call | solution.py:747
